TPU v7x, 128 devices: a whole 4x4x4 slice. The times are simulated.
128 devices in a mesh: ep: 16 (over z, x), tp: 8 (over y, core).
Axes of the slice: x: 4, y: 4, z: 4, core: 2. Of those that a mesh axis runs over, the one named last changes fastest.
Arguments:
- tokens: bfloat16 [2048, 2880], P('ep'), may hold values from -6 to 6
- seq_lengths: int32 [16, 2], replicated, may hold values from 0 to 128, as said below
- expert_ids: int32 [2048, 4], P('ep'), may hold values from 0 to 15, all different within a row; in each aligned block of 128 rows (0 to 127, 128 to 255, ...) at most 48 rows name the same one
- first_gain: float32 [2880], replicated, may hold values from 0.5 to 1.5
- query_weight: bfloat16 [2880, 4096], P(None, 'tp'), may hold values from -0.109375 to 0.109375
- key_matrix: bfloat16 [2880, 512], P(None, 'tp'), may hold values from -0.109375 to 0.109375
- value_matrix: bfloat16 [2880, 512], P(None, 'tp'), may hold values from -0.109375 to 0.109375
- query_bias: float32 [4096], P('tp'), may hold values from -2 to 2
- key_offset_bias: float32 [512], P('tp'), may hold values from -2 to 2
- value_offset_bias: float32 [512], P('tp'), may hold values from -2 to 2
- head_sink_logits: float32 [64], P('tp'), may hold values from 1 to 4
- output_weight: bfloat16 [4096, 2880], P('tp'), may hold values from -0.75 to 0.75
- output_bias: float32 [2880], replicated, may hold values from -2 to 2
- second_gain: float32 [2880], replicated, may hold values from 0.5 to 1.5
- router_weight: bfloat16 [2880, 16], replicated, may hold values from -0.0546875 to 0.0546875
- router_bias: float32 [16], replicated, may hold values from -1 to 1
- expert_gateup: bfloat16 [16, 2, 2880, 2880], P('ep', None, None, 'tp'), may hold values from -0.109375 to 0.109375
- gateup_bias: float32 [16, 2, 2880], P('ep', None, 'tp'), may hold values from -1 to 1
- expert_down: bfloat16 [16, 2880, 2880], P('ep', 'tp'), may hold values from -0.109375 to 0.109375
- down_bias: float32 [16, 2880], P('ep'), may hold values from -1 to 1
- cotangent: bfloat16 [2048, 2880], P('ep'), may hold values from -6 to 6
Outputs:
- layer_output: bfloat16 [2048, 2880], P('ep')
- grad_tokens: float32 [2048, 2880], P('ep')
- grad_first_gain: float32 [2880], replicated
- grad_query_weight: float32 [2880, 4096], P(None, 'tp')
- grad_key_weight: float32 [2880, 512], P(None, 'tp')
- grad_value_weight: float32 [2880, 512], P(None, 'tp')
- grad_query_bias: float32 [4096], P('tp')
- grad_key_bias: float32 [512], P('tp')
- grad_value_bias: float32 [512], P('tp')
- grad_sink_logits: float32 [64], P('tp')
- grad_output_weight: float32 [4096, 2880], P('tp')
- grad_output_bias: float32 [2880], replicated
- grad_second_gain: float32 [2880], replicated
- grad_router_weight: float32 [2880, 16], replicated
- grad_router_bias: float32 [16], replicated
- grad_expert_gateup: float32 [16, 2, 2880, 2880], P('ep', None, None, 'tp')
- grad_gateup_bias: float32 [16, 2, 2880], P('ep', None, 'tp')
- grad_expert_down: float32 [16, 2880, 2880], P('ep', 'tp')
- grad_down_bias: float32 [16, 2880], P('ep')
Inputs may be any that keep to these rules, and one draw needn't show every extreme that they name: `seq_lengths`: for each token group, entry 0 is more than half of 128 and the two entries sum to at most 128; the rows after both sequences form a third one. Some group holds a single sequence of 128 tokens. `expert_ids`: each row names 4 different experts; among the 128 rows of one token group no expert is named more than 48 times, a bound that some block reaches.
All inputs are finite; a program needn't handle non-finite values.
Results may differ from a plain program's by a relative error of at most 0.023.
Values may be sent and summed in bfloat16 or wider, within the bound.
A program may use at most 192 MiB of HBM per device.

v0:
```python
from functools import partial

import jax
import jax.numpy as jnp
from jax import lax
from jax.sharding import PartitionSpec as P

HEAD_SIZE = 64


EPS = 1e-05
THETA = 150000.0
LIMIT = 7.0
ALPHA = 1.702
NEGATIVE = -1e30


def padded_to(lines, length):
    spare = -lines.shape[0] % length
    if not spare:
        return lines
    return jnp.concatenate([lines, jnp.zeros((spare, *lines.shape[1:]), lines.dtype)])


def total_of(array, axis):
    lines = array.reshape(-1, *array.shape[1:][-1:])
    own = lax.psum_scatter(
        padded_to(lines, lax.axis_size(axis)), axis, scatter_dimension=0, tiled=True
    )
    whole = lax.all_gather(own, axis).reshape(-1, *lines.shape[1:])
    return lax.slice_in_dim(whole, 0, len(lines)).reshape(array.shape)


def product(left, right):
    return jnp.dot(left, right, preferred_element_type=jnp.float32)


def contract_rows(left, right):
    return lax.dot_general(
        left, right, (((0,), (0,)), ((), ())), preferred_element_type=jnp.float32
    )


def against_rows(left, right):
    return lax.dot_general(
        left, right, (((1,), (1,)), ((), ())), preferred_element_type=jnp.float32
    )


def rms_norm(value_rows, gain_vector):
    return (
        value_rows
        * lax.rsqrt(jnp.mean(value_rows * value_rows, axis=-1, keepdims=True) + EPS)
        * gain_vector
    )


def angles_of(positions, head_width):
    exponent = jnp.arange(head_width // 2, dtype=jnp.float32) * (2.0 / head_width)
    frequency = jnp.power(THETA, -exponent)
    return positions.astype(jnp.float32)[:, None] * frequency[None, :]


def apply_rotary(value_rows, rotary_angles):
    half_width = value_rows.shape[-1] // 2
    cosine = jnp.cos(rotary_angles)[:, None, :]
    sine_part = jnp.sin(rotary_angles)[:, None, :]
    first_half = value_rows[..., :half_width]
    second_half = value_rows[..., half_width:]
    return jnp.concatenate(
        [
            first_half * cosine - second_half * sine_part,
            second_half * cosine + first_half * sine_part,
        ],
        axis=-1,
    )


def layout(lengths_row, count_of_rows):
    row_index = jnp.arange(count_of_rows, dtype=jnp.int32)
    first_end = lengths_row[0]
    second_end = lengths_row[0] + lengths_row[1]
    document = (row_index >= first_end).astype(jnp.int32) + (row_index >= second_end).astype(
        jnp.int32
    )
    doc_start = jnp.where(document == 0, 0, jnp.where(document == 1, first_end, second_end))
    return (row_index - doc_start, document)


def log_totals(scores, sink_logit_column):
    highest = jnp.maximum(jnp.max(scores, axis=-1), sink_logit_column)
    total = jnp.exp(sink_logit_column - highest) + jnp.sum(
        jnp.exp(scores - highest[..., None]), axis=-1
    )
    return highest + jnp.log(total)


def gate_weights(logits, chosen):
    picked = jnp.sum(chosen * logits[:, None, :], axis=-1)
    highest = jnp.max(picked, axis=-1, keepdims=True)
    raised = jnp.exp(picked - highest)
    return raised / jnp.sum(raised, axis=-1, keepdims=True)


def activate(gate_pre, up_pre):
    capped_gate = LIMIT - jax.nn.softplus(LIMIT - gate_pre)
    capped_up = LIMIT * jnp.tanh(up_pre / LIMIT)
    return (capped_up + 1.0) * capped_gate * jax.nn.sigmoid(ALPHA * capped_gate)


def send_out(rows_block, tp_place, tp_count):
    model_width = rows_block.shape[2]
    share = rows_block.shape[1] // tp_count
    piece = lax.dynamic_slice_in_dim(rows_block, tp_place * share, share, 1)
    moved = lax.all_to_all(piece, "ep", split_axis=0, concat_axis=0, tiled=True)
    return lax.all_gather(moved, "tp", axis=1, tiled=True).reshape(-1, model_width)


def send_home(partial_rows, ep_count, capacity):
    model_width = partial_rows.shape[1]
    blocks = partial_rows.reshape(ep_count, capacity, model_width)
    shares = lax.psum_scatter(blocks, "tp", scatter_dimension=1, tiled=True).astype(jnp.bfloat16)
    moved = lax.all_to_all(shares, "ep", split_axis=0, concat_axis=0, tiled=True)
    return lax.all_gather(moved, "tp", axis=1, tiled=True).reshape(-1, model_width)


def shards(
    tokens,
    seq_lengths,
    expert_ids,
    first_gain,
    query_weight,
    key_matrix,
    value_matrix,
    query_bias,
    key_offset_bias,
    value_offset_bias,
    head_sink_logits,
    output_weight,
    output_bias,
    second_gain,
    router_weight,
    router_bias,
    expert_gateup,
    gateup_bias,
    expert_down,
    down_bias,
    cotangent,
):
    ep_count = lax.axis_size("ep")
    tp_count = lax.axis_size("tp")
    tp_place = lax.axis_index("tp")
    ep_place = lax.axis_index("ep")
    local_rows, model_width = tokens.shape
    top_count = expert_ids.shape[1]
    experts = router_weight.shape[1]
    capacity = tp_count * max(1, 3 * local_rows * top_count // (2 * experts * tp_count))
    heads_local = query_weight.shape[1] // HEAD_SIZE
    kv_local = key_matrix.shape[1] // HEAD_SIZE
    heads_per_group = heads_local // kv_local
    score_scale = HEAD_SIZE ** (-0.5)
    lengths_row = lax.dynamic_index_in_dim(seq_lengths, ep_place, 0, keepdims=False)
    positions, document = layout(lengths_row, local_rows)
    rotary_angles = angles_of(positions, HEAD_SIZE)
    row_index = jnp.arange(local_rows)
    allowed = (document[:, None] == document[None, :]) & (row_index[None, :] <= row_index[:, None])
    sink_logit_column = head_sink_logits.reshape(kv_local, heads_per_group)[:, :, None]
    inputs = tokens.astype(jnp.float32)
    normalized_input, first_back = jax.vjp(rms_norm, inputs, first_gain)
    normed_low = normalized_input.astype(jnp.bfloat16)
    query_unrotated = product(normed_low, query_weight) + query_bias
    key_unrotated = product(normed_low, key_matrix) + key_offset_bias
    value_low = (
        (product(normed_low, value_matrix) + value_offset_bias)
        .astype(jnp.bfloat16)
        .reshape(local_rows, kv_local, HEAD_SIZE)
    )

    def rotate_both(query_in, key_in):
        return (
            apply_rotary(query_in.reshape(local_rows, heads_local, HEAD_SIZE), rotary_angles),
            apply_rotary(key_in.reshape(local_rows, kv_local, HEAD_SIZE), rotary_angles),
        )

    rotated, rotate_back = jax.vjp(rotate_both, query_unrotated, key_unrotated)
    query_low = (
        rotated[0].astype(jnp.bfloat16).reshape(local_rows, kv_local, heads_per_group, HEAD_SIZE)
    )
    key_low = rotated[1].astype(jnp.bfloat16)

    def masked_scores():
        raw_scores = (
            jnp.einsum("qhgd,khd->hgqk", query_low, key_low, preferred_element_type=jnp.float32)
            * score_scale
        )
        return jnp.where(allowed[None, None], raw_scores, NEGATIVE)

    scores = masked_scores()
    log_total = log_totals(scores, sink_logit_column)
    probs_low = jnp.exp(scores - log_total[..., None]).astype(jnp.bfloat16)
    head_values = jnp.einsum(
        "hgqk,khd->qhgd", probs_low, value_low, preferred_element_type=jnp.float32
    )
    heads_low = head_values.reshape(local_rows, heads_local * HEAD_SIZE).astype(jnp.bfloat16)
    attended = total_of(product(heads_low, output_weight), "tp") + output_bias
    mixed = inputs + attended
    second, second_back = jax.vjp(rms_norm, mixed, second_gain)
    second_low = second.astype(jnp.bfloat16)
    logits = product(second_low, router_weight) + router_bias
    chosen_int = (
        expert_ids[:, :, None] == jnp.arange(experts, dtype=jnp.int32)[None, None, :]
    ).astype(jnp.int32)
    chosen = chosen_int.astype(jnp.float32)
    gate_share, gate_back = jax.vjp(partial(gate_weights, chosen=chosen), logits)
    flat_routes = chosen_int.reshape(local_rows * top_count, experts)
    before = jnp.cumsum(flat_routes, axis=0, dtype=jnp.int32) - flat_routes
    slot_rank = jnp.sum(before * flat_routes, axis=1, dtype=jnp.int32).reshape(
        local_rows, top_count
    )
    slot_code = expert_ids * capacity + slot_rank
    selector = (
        slot_code[:, :, None] == jnp.arange(experts * capacity, dtype=jnp.int32)[None, None, :]
    ).astype(jnp.bfloat16)
    placing = jnp.sum(selector, axis=1)
    buffer = jnp.einsum(
        "tc,td->cd", placing, second_low, preferred_element_type=jnp.float32
    ).astype(jnp.bfloat16)
    expert_rows = send_out(buffer.reshape(experts, capacity, model_width), tp_place, tp_count)
    gate_pre = product(expert_rows, expert_gateup[0, 0]) + gateup_bias[0, 0]
    up_pre = product(expert_rows, expert_gateup[0, 1]) + gateup_bias[0, 1]
    hidden, hidden_back = jax.vjp(activate, gate_pre, up_pre)
    hidden_low = hidden.astype(jnp.bfloat16)
    first_slice = jnp.where(tp_place == 0, 1.0, 0.0).astype(jnp.float32)
    partial_out = product(hidden_low, expert_down[0]) + first_slice * down_bias[0]
    results = send_home(partial_out, ep_count, capacity)
    picked = jnp.einsum("tkc,cd->tkd", selector, results, preferred_element_type=jnp.float32)
    moe_out = jnp.sum(gate_share[:, :, None] * picked, axis=1)
    layer_output = (mixed + moe_out).astype(jnp.bfloat16)
    grad_final = cotangent.astype(jnp.float32)
    grad_gates = jnp.sum(grad_final[:, None, :] * picked, axis=-1)
    gated = (gate_share[:, :, None] * grad_final[:, None, :]).astype(jnp.bfloat16)
    grad_results = jnp.einsum(
        "tkc,tkd->cd", selector, gated, preferred_element_type=jnp.float32
    ).astype(jnp.bfloat16)
    grad_rows = send_out(grad_results.reshape(experts, capacity, model_width), tp_place, tp_count)
    grad_down_bias = jnp.sum(grad_rows.astype(jnp.float32), axis=0)[None]
    grad_down = contract_rows(hidden_low, grad_rows)[None]
    grad_hidden = against_rows(grad_rows, expert_down[0])
    grad_gate_pre, grad_up_pre = hidden_back(grad_hidden)
    grad_gate_low = grad_gate_pre.astype(jnp.bfloat16)
    grad_up_low = grad_up_pre.astype(jnp.bfloat16)
    grad_gateup = jnp.stack(
        [contract_rows(expert_rows, grad_gate_low), contract_rows(expert_rows, grad_up_low)]
    )[None]
    grad_gateup_bias = jnp.stack(
        [
            jnp.sum(grad_gate_low.astype(jnp.float32), axis=0),
            jnp.sum(grad_up_low.astype(jnp.float32), axis=0),
        ]
    )[None]
    grad_inputs = against_rows(grad_gate_low, expert_gateup[0, 0]) + against_rows(
        grad_up_low, expert_gateup[0, 1]
    )
    returned_grads = send_home(grad_inputs, ep_count, capacity)
    grad_second = jnp.einsum(
        "tkc,cd->td", selector, returned_grads, preferred_element_type=jnp.float32
    )
    (grad_logits,) = gate_back(grad_gates)
    router_values = router_weight.astype(jnp.float32)
    grad_second = grad_second + lax.dot_general(
        grad_logits, router_values, (((1,), (1,)), ((), ()))
    )
    grad_router_weight = lax.dot_general(
        second_low.astype(jnp.float32), grad_logits, (((0,), (0,)), ((), ()))
    )
    grad_router_bias = jnp.sum(grad_logits, axis=0)
    grad_mixed_norm, grad_second_gain = second_back(grad_second)
    grad_mixed = grad_final + grad_mixed_norm
    grad_attended = grad_mixed.astype(jnp.bfloat16)
    grad_output_bias = jnp.sum(grad_attended.astype(jnp.float32), axis=0)
    grad_output_weight = contract_rows(heads_low, grad_attended)
    grad_heads = (
        against_rows(grad_attended, output_weight)
        .astype(jnp.bfloat16)
        .reshape(local_rows, kv_local, heads_per_group, HEAD_SIZE)
    )
    probs_full = jnp.exp(masked_scores() - log_total[..., None])
    grad_probs = jnp.einsum(
        "qhgd,khd->hgqk", grad_heads, value_low, preferred_element_type=jnp.float32
    )
    row_delta = jnp.sum(probs_full * grad_probs, axis=-1)
    grad_scores = (probs_full * (grad_probs - row_delta[..., None])).astype(jnp.bfloat16)
    grad_sinks = -jnp.sum(jnp.exp(sink_logit_column - log_total) * row_delta, axis=-1).reshape(-1)
    grad_values_low = (
        jnp.einsum("hgqk,qhgd->khd", probs_low, grad_heads, preferred_element_type=jnp.float32)
        .astype(jnp.bfloat16)
        .reshape(local_rows, kv_local * HEAD_SIZE)
    )
    grad_query_rot = (
        jnp.einsum("hgqk,khd->qhgd", grad_scores, key_low, preferred_element_type=jnp.float32)
        * score_scale
    )
    grad_key_rot = (
        jnp.einsum("hgqk,qhgd->khd", grad_scores, query_low, preferred_element_type=jnp.float32)
        * score_scale
    )
    grad_query_pre, grad_key_pre = rotate_back(
        (grad_query_rot.reshape(local_rows, heads_local, HEAD_SIZE), grad_key_rot)
    )
    grad_query_low = grad_query_pre.astype(jnp.bfloat16)
    grad_key_low = grad_key_pre.astype(jnp.bfloat16)
    grad_query_weight = contract_rows(normed_low, grad_query_low)
    grad_key_weight = contract_rows(normed_low, grad_key_low)
    grad_value_weight = contract_rows(normed_low, grad_values_low)
    grad_query_bias = jnp.sum(grad_query_low.astype(jnp.float32), axis=0)
    grad_key_bias = jnp.sum(grad_key_low.astype(jnp.float32), axis=0)
    grad_value_bias = jnp.sum(grad_values_low.astype(jnp.float32), axis=0)
    local_normed_grad = (
        against_rows(grad_query_low, query_weight)
        + against_rows(grad_key_low, key_matrix)
        + against_rows(grad_values_low, value_matrix)
    )
    grad_normed = total_of(local_normed_grad.astype(jnp.bfloat16), "tp").astype(jnp.float32)
    grad_inputs_norm, grad_first_gain = first_back(grad_normed)
    grad_tokens = grad_mixed + grad_inputs_norm
    summed_weights = (
        lax.psum(grad_query_weight.astype(jnp.bfloat16), "ep").astype(jnp.float32),
        lax.psum(grad_key_weight.astype(jnp.bfloat16), "ep").astype(jnp.float32),
        lax.psum(grad_value_weight.astype(jnp.bfloat16), "ep").astype(jnp.float32),
        lax.psum(grad_output_weight.astype(jnp.bfloat16), "ep").astype(jnp.float32),
        lax.psum(grad_query_bias.astype(jnp.bfloat16), "ep").astype(jnp.float32),
        lax.psum(grad_key_bias.astype(jnp.bfloat16), "ep").astype(jnp.float32),
        lax.psum(grad_value_bias.astype(jnp.bfloat16), "ep").astype(jnp.float32),
        lax.psum(grad_sinks.astype(jnp.bfloat16), "ep").astype(jnp.float32),
        lax.psum(grad_first_gain.astype(jnp.bfloat16), "ep").astype(jnp.float32),
        lax.psum(grad_second_gain.astype(jnp.bfloat16), "ep").astype(jnp.float32),
        lax.psum(grad_output_bias.astype(jnp.bfloat16), "ep").astype(jnp.float32),
        lax.psum(grad_router_weight.astype(jnp.bfloat16), "ep").astype(jnp.float32),
        lax.psum(grad_router_bias.astype(jnp.bfloat16), "ep").astype(jnp.float32),
    )
    return (
        layer_output,
        grad_tokens,
        summed_weights[8],
        summed_weights[0],
        summed_weights[1],
        summed_weights[2],
        summed_weights[4],
        summed_weights[5],
        summed_weights[6],
        summed_weights[7],
        summed_weights[3],
        summed_weights[10],
        summed_weights[9],
        summed_weights[11],
        summed_weights[12],
        grad_gateup,
        grad_gateup_bias,
        grad_down,
        grad_down_bias,
    )


def solution(mesh):
    in_specs = (
        P("ep", None),
        P(),
        P("ep", None),
        P(),
        P(None, "tp"),
        P(None, "tp"),
        P(None, "tp"),
        P("tp"),
        P("tp"),
        P("tp"),
        P("tp"),
        P("tp", None),
        P(),
        P(),
        P(),
        P(),
        P("ep", None, None, "tp"),
        P("ep", None, "tp"),
        P("ep", "tp", None),
        P("ep", None),
        P("ep", None),
    )
    out_specs = (
        P("ep", None),
        P("ep", None),
        P(),
        P(None, "tp"),
        P(None, "tp"),
        P(None, "tp"),
        P("tp"),
        P("tp"),
        P("tp"),
        P("tp"),
        P("tp", None),
        P(),
        P(),
        P(),
        P(),
        P("ep", None, None, "tp"),
        P("ep", None, "tp"),
        P("ep", "tp", None),
        P("ep", None),
    )
    return jax.shard_map(shards, mesh=mesh, in_specs=in_specs, out_specs=out_specs, check_vma=False)
```

profile of v0, /device:TPU:1, one launch (start us, length us, event | category | flops | bytes accessed | tf_op | source)
XLA Modules:
  0.0 620.6 jit_solution(14865897631660651375)
XLA Ops:
  24.6 33.0 %reduce-scatter.5.cloned.1.call-done = f32[16,2880]{1,0:T(8,128)} async-done(((f32[128,2880]{1,0:T(8,128)}), f32[16,2880]{1,0:T(8,128)}) %reduce-scatter.5.cloned.1.call-update) | async-done | bytes 184336 | tf_op jit(solution)/shard_map/reduce_scatter | solution.py:27
  69.6 16.3 %all-gather.16.cloned.1.call-done = f32[128,2880]{1,0:T(8,128)} async-done(((f32[16,2880]{1,0:T(8,128)}), f32[128,2880]{1,0:T(8,128)}) %all-gather.16.cloned.1.call-update) | async-done | bytes 1474576 | tf_op jit(solution)/shard_map/all_gather | solution.py:30
  90.6 5.5 bitcast_convert_fusion
  96.1 6.5 %copy.217 = bf16[768,2880]{1,0:T(8,128)(2,1)} copy(bf16[768,2880]{0,1:T(8,128)(2,1)} %bitcast_convert_fusion) | data formatting | bytes 8847360 | tf_op jit(solution)/shard_map/convert_element_type | solution.py:244
  104.2 20.1 %all_to_all.20 = bf16[16,6,2880]{2,1,0:T(8,128)(2,1)S(1)} all-to-all(bf16[16,6,2880]{2,1,0:T(8,128)(2,1)S(1)} %constant_dynamic-slice_fusion), channel_id=1, replica_groups=mesh['ep'=16,'tp'=8] {'ep'}, dimensions={0} | all-to-all | bytes 1105920 | tf_op jit(solution)/shard_map/all_to_all | solution.py:115
  130.8 6.6 %copy.205 = bf16[768,2880]{1,0:T(8,128)(2,1)} copy(bf16[768,2880]{0,1:T(8,128)(2,1)} %convolution_convert_fusion) | data formatting | bytes 8847360 | tf_op jit(solution)/shard_map/convert_element_type | solution.py:227
  139.0 15.6 %all_to_all.21 = bf16[16,6,2880]{2,1,0:T(8,128)(2,1)S(1)} all-to-all(bf16[16,6,2880]{2,1,0:T(8,128)(2,1)S(1)} %constant_dynamic-slice_fusion.1), channel_id=1, replica_groups=mesh['ep'=16,'tp'=8] {'ep'}, dimensions={0} | all-to-all | bytes 1105920 | tf_op jit(solution)/shard_map/all_to_all | solution.py:115
  164.9 27.0 %all-gather.8.cloned.1.call-done = bf16[16,48,2880]{2,0,1:T(8,128)(2,1)} async-done(((bf16[16,6,2880]{2,0,1:T(8,128)(2,1)}), bf16[16,48,2880]{2,0,1:T(8,128)(2,1)}) %all-gather.8.cloned.1.call-update) | async-done | bytes 4423696 | tf_op jit(solution)/shard_map/all_gather | solution.py:116
  206.3 6.4 %convolution_add_fusion.1 = f32[768,2880]{0,1:T(8,128)} fusion(f32[2880]{0:T(1024)S(1)} %multiply_reduce_fusion.7, bf16[1,360,2880]{2,1,0:T(8,128)(2,1)S(1)} %copy-done.87, f32[768,360]{0,1:T(8,128)S(1)} %get-tuple-element.188, f32[768,360]{0,1:T(8,128)S(1)} %fusion.39), kind=kOutput, calls=%fused_computation.7 | convolution fusion | flops 1599160320 | bytes 13144320 | tf_op jit(solution)/shard_map/dot_general | solution.py:35
  212.8 9.5 %copy.208 = f32[768,2880]{1,0:T(8,128)} copy(f32[768,2880]{0,1:T(8,128)} %convolution_add_fusion.1) | data formatting | bytes 17694720 | tf_op jit(solution)/shard_map/add | solution.py:234
  222.2 10.0 %copy.209 = f32[16,48,2880]{2,0,1:T(8,128)} copy(f32[16,48,2880]{2,1,0:T(8,128)} %bitcast.183) | data formatting | bytes 17694720 | tf_op jit(solution)/shard_map/reshape | solution.py:121
  236.8 8.1 %convolution_add_fusion = f32[768,2880]{0,1:T(8,128)} fusion(f32[768,2880]{0,1:T(8,128)S(1)} %fusion.6, bf16[768,360]{0,1:T(8,128)(2,1)S(1)} %copy-done.26, bf16[1,2,2880,360]{2,3,1,0:T(8,128)(2,1)} %param.37), kind=kOutput, calls=%fused_computation.6 | convolution fusion | flops 1594736640 | bytes 20367360 | tf_op jit(solution)/shard_map/dot_general | solution.py:45
  244.9 9.7 %copy.220 = f32[768,2880]{1,0:T(8,128)} copy(f32[768,2880]{0,1:T(8,128)} %convolution_add_fusion) | data formatting | bytes 17694720 | tf_op jit(solution)/shard_map/add | solution.py:261
  254.6 10.2 %copy.221 = f32[16,48,2880]{2,0,1:T(8,128)} copy(f32[16,48,2880]{2,1,0:T(8,128)} %bitcast.184) | data formatting | bytes 17694720 | tf_op jit(solution)/shard_map/reshape | solution.py:121
  264.9 22.1 %reduce-scatter.7.cloned.1.call-done = f32[16,6,2880]{2,0,1:T(8,128)} async-done(((f32[16,48,2880]{2,0,1:T(8,128)}), f32[16,6,2880]{2,0,1:T(8,128)}) %reduce-scatter.7.cloned.1.call-update) | async-done | bytes 1105936 | tf_op jit(solution)/shard_map/reduce_scatter | solution.py:122
  288.4 18.7 %all_to_all.22 = bf16[16,6,2880]{2,1,0:T(8,128)(2,1)S(1)} all-to-all(bf16[16,6,2880]{2,1,0:T(8,128)(2,1)S(1)} %copy.210), channel_id=1, replica_groups=mesh['ep'=16,'tp'=8] {'ep'}, dimensions={0} | all-to-all | bytes 1105920 | tf_op jit(solution)/shard_map/all_to_all | solution.py:123
  308.1 36.5 %reduce-scatter.9.cloned.1.call-done = f32[16,6,2880]{2,0,1:T(8,128)} async-done(((f32[16,48,2880]{2,0,1:T(8,128)}), f32[16,6,2880]{2,0,1:T(8,128)}) %reduce-scatter.9.cloned.1.call-update) | async-done | bytes 1105936 | tf_op jit(solution)/shard_map/reduce_scatter | solution.py:122
  346.0 18.8 %all_to_all.23 = bf16[16,6,2880]{2,1,0:T(8,128)(2,1)S(1)} all-to-all(bf16[16,6,2880]{2,1,0:T(8,128)(2,1)S(1)} %copy.222), channel_id=1, replica_groups=mesh['ep'=16,'tp'=8] {'ep'}, dimensions={0} | all-to-all | bytes 1105920 | tf_op jit(solution)/shard_map/all_to_all | solution.py:123
  365.7 15.2 %all-gather.10.cloned.1.call-done = bf16[16,48,2880]{2,0,1:T(8,128)(2,1)} async-done(((bf16[16,6,2880]{2,0,1:T(8,128)(2,1)}), bf16[16,48,2880]{2,0,1:T(8,128)(2,1)}) %all-gather.10.cloned.1.call-update) | async-done | bytes 4423696 | tf_op jit(solution)/shard_map/all_gather | solution.py:124
  384.1 5.9 multiply_reduce_fusion
  393.9 22.3 %all-gather.14.cloned.1.call-done = bf16[16,48,2880]{2,0,1:T(8,128)(2,1)} async-done(((bf16[16,6,2880]{2,0,1:T(8,128)(2,1)}), bf16[16,48,2880]{2,0,1:T(8,128)(2,1)}) %all-gather.14.cloned.1.call-update) | async-done | bytes 4423696 | tf_op jit(solution)/shard_map/all_gather | solution.py:124
  470.7 13.6 %all-gather.1 = bf16[128,2880]{1,0:T(8,128)(2,1)S(1)} all-gather(bf16[16,2880]{1,0:T(8,128)(2,1)} %reduce-scatter.11.cloned.1.call-done), channel_id=3, replica_groups=mesh['ep'=16,'tp'=8] {'tp'}, dimensions={0}, use_global_device_ids=true | all-gather | bytes 829440 | tf_op jit(solution)/shard_map/all_gather | solution.py:30
  487.2 61.7 %all-reduce.4 = (bf16[2880]{0:T(1024)(128)(2,1)S(1)}, bf16[512]{0:T(512)(128)(2,1)S(1)}, bf16[64]{0:T(256)(128)(2,1)S(1)}, bf16[64]{0:T(256)(128)(2,1)S(1)}, bf1...) all-reduce(bf16[2880]{0:T(1024)(128)(2,1)S(1)} %get-tuple-element.1, ...), channel_id=1, replica_groups=mesh['ep'=16,'tp'=8] {'ep'}, use_global_device_ids=true, to_apply=%region_25.26 | all-reduce | flops 9304 | bytes 37216 | tf_op jit(solution)/shard_map/psum | solution.py:335
  559.7 40.5 %all-reduce.8.cloned.1.call-done = (bf16[2880,512]{1,0:T(8,128)(2,1)}, bf16[2880,64]{0,1:T(8,128)(2,1)}, bf16[2880,64]{0,1:T(8,128)(2,1)}, bf16[512,2880]{0,1:T(8,128)(2,1)}, bf16[2880,16]{0,1:T(8,128)(2,1)}) async-done(((bf16[2880,512]{1,0:T(8,128)(2,1)}, bf16[2880,64]{0,1:T(8,128)(2,1)}, bf16[2880,64]{0,1:T(8,128)(2,1)}, bf16[512,2880]{0,1:T(8,128)(2,1)}, bf16[2880,16]{0,1:T(8,128)(2,1)}), ...) | async-done | bytes 6727696 | tf_op jit(solution)/shard_map/psum | solution.py:327
  (355 shorter events, 163.9 us)
Async XLA Ops:
  7.2 15.1 %copy-start = (bf16[512,2880]{0,1:T(8,128)(2,1)S(1)}, bf16[512,2880]{0,1:T(8,128)(2,1)}, u32[]{:S(2)}) copy-start(bf16[512,2880]{0,1:T(8,128)(2,1)} %param.32) | copy-start | bytes 8847364
  7.2 50.4 %reduce-scatter.5.cloned.1.call-start = ((), (), s32[]{:S(2)}) async-start(), calls=%async_computation.8 | async-start | bytes 1695744 | tf_op jit(solution)/shard_map/reduce_scatter | solution.py:27
  7.3 9.5 %copy-start.64 = (f32[32]{0:T(128)}, f32[32]{0:T(128)S(1)}, u32[]{:S(2)}) copy-start(f32[32]{0:T(128)S(1)} %negate_power_fusion) | copy-start | bytes 388
  24.6 61.3 %all-gather.16.cloned.1.call-start = ((), (), s32[]{:S(2)}) async-start(), calls=%async_computation.16 | async-start | bytes 1695744 | tf_op jit(solution)/shard_map/all_gather | solution.py:30
  57.6 99.0 %all-gather.12.cloned.1.call-start = ((), (), s32[]{:S(2)}) async-start(), calls=%async_computation.12 | async-start | bytes 5087232 | tf_op jit(solution)/shard_map/all_gather | solution.py:116
  64.7 21.1 %copy-start.56 = (f32[2880]{0:T(1024)S(1)}, f32[2880]{0:T(1024)}, u32[]{:S(2)}) copy-start(f32[2880]{0:T(1024)} %param.33) | copy-start | bytes 34564
  69.6 18.3 %copy-start.40 = (f32[2880]{0:T(1024)S(1)}, f32[2880]{0:T(1024)}, u32[]{:S(2)}) copy-start(f32[2880]{0:T(1024)} %param.34) | copy-start | bytes 34564
  125.2 66.7 %all-gather.8.cloned.1.call-start = ((), (), s32[]{:S(2)}) async-start(), calls=%async_computation.9 | async-start | bytes 5087232 | tf_op jit(solution)/shard_map/all_gather | solution.py:116
  139.0 17.0 %copy-start.71 = (f32[1,2,360]{2,1,0:T(2,128)S(1)}, f32[1,2,360]{2,1,0:T(2,128)}, u32[]{:S(2)}) copy-start(f32[1,2,360]{2,1,0:T(2,128)} %param.38) | copy-start | bytes 8644
  139.0 17.6 %copy-start.57 = (f32[1,2880]{1,0:T(1,128)S(1)}, f32[1,2880]{1,0:T(1,128)}, u32[]{:S(2)}) copy-start(f32[1,2880]{1,0:T(1,128)} %param.40) | copy-start | bytes 34564
  155.4 131.5 %reduce-scatter.7.cloned.1.call-start = ((), (), s32[]{:S(2)}) async-start(), calls=%async_computation.10 | async-start | bytes 10174464 | tf_op jit(solution)/shard_map/reduce_scatter | solution.py:122
  164.9 30.2 %copy-start.75 = (f32[360]{0:T(512)S(1)}, f32[360]{0:T(512)}, u32[]{:S(2)}) copy-start(f32[360]{0:T(512)} %get-tuple-element.141) | copy-start | bytes 4324
  232.3 112.3 %reduce-scatter.9.cloned.1.call-start = ((), (), s32[]{:S(2)}) async-start(), calls=%async_computation.13 | async-start | bytes 10174464 | tf_op jit(solution)/shard_map/reduce_scatter | solution.py:122
  264.8 116.1 %all-gather.10.cloned.1.call-start = ((), (), s32[]{:S(2)}) async-start(), calls=%async_computation.11 | async-start | bytes 5087232 | tf_op jit(solution)/shard_map/all_gather | solution.py:124
  308.1 108.1 %all-gather.14.cloned.1.call-start = ((), (), s32[]{:S(2)}) async-start(), calls=%async_computation.14 | async-start | bytes 5087232 | tf_op jit(solution)/shard_map/all_gather | solution.py:124
  365.7 105.0 %reduce-scatter.11.cloned.1.call-start = ((), (), s32[]{:S(2)}) async-start(), calls=%async_computation.15 | async-start | bytes 847872 | tf_op jit(solution)/shard_map/reduce_scatter | solution.py:27
  365.7 18.4 %copy-start.74 = (f32[128,4]{0,1:T(4,128)S(1)}, f32[128,4]{0,1:T(4,128)}, u32[]{:S(2)}) copy-start(f32[128,4]{0,1:T(4,128)} %copy-done.73) | copy-start | bytes 6148
  393.9 26.2 %copy-start.51 = (bf16[128,16]{0,1:T(8,128)(2,1)}, bf16[128,16]{0,1:T(8,128)(2,1)S(1)}, u32[]{:S(2)}) copy-start(bf16[128,16]{0,1:T(8,128)(2,1)S(1)} %get-tuple-element.140) | copy-start | bytes 12292
  437.4 162.9 %all-reduce.8.cloned.1.call-start = ((), (), s32[]{:S(2)}) async-start(), calls=%async_computation.17 | async-start | bytes 13492224 | tf_op jit(solution)/shard_map/psum | solution.py:327
  470.3 16.9 %copy-start.54 = (bf16[2880]{0:T(1024)(128)(2,1)S(1)}, bf16[2880]{0:T(1024)(128)(2,1)}, u32[]{:S(2)}) copy-start(bf16[2880]{0:T(1024)(128)(2,1)} %get-tuple-element.135) | copy-start | bytes 17284
  470.3 16.9 %copy-start.55 = (bf16[2880]{0:T(1024)(128)(2,1)S(1)}, bf16[2880]{0:T(1024)(128)(2,1)}, u32[]{:S(2)}) copy-start(bf16[2880]{0:T(1024)(128)(2,1)} %get-tuple-element.160) | copy-start | bytes 17284
  470.3 16.9 %copy-start.72 = (bf16[64]{0:T(256)(128)(2,1)S(1)}, bf16[64]{0:T(256)(128)(2,1)}, u32[]{:S(2)}) copy-start(bf16[64]{0:T(256)(128)(2,1)} %get-tuple-element.192) | copy-start | bytes 388
  470.3 16.9 %copy-start.77 = (bf16[16]{0:T(256)(128)(2,1)S(1)}, bf16[16]{0:T(256)(128)(2,1)}, u32[]{:S(2)}) copy-start(bf16[16]{0:T(256)(128)(2,1)} %get-tuple-element.139) | copy-start | bytes 100
  470.3 83.0 %copy-start.82 = (f32[128]{0:T(128)S(1)}, f32[128]{0:T(128)}, u32[]{:S(2)}) copy-start(f32[128]{0:T(128)} %copy-done.81) | copy-start | bytes 1540
  (88 other events, 281.4 us)
Sparse Core Ops, SparseCore 0:
  24.7 32.8 reduce-scatter.4
  59.3 26.5 all-gather.15
  125.3 30.9 all-gather.11
  158.4 33.4 all-gather.7
  232.4 54.5 reduce-scatter.6
  289.4 55.1 reduce-scatter.8
  346.8 34.0 all-gather.9
  382.6 33.4 all-gather.13
  437.5 28.1 reduce-scatter.10
  470.8 129.3 all-reduce.7
where the time goes:
time: 630 us; the launch traced here: 621 us
  waiting for transfers between devices  213 us (34%)
  blocking collectives  148 us (23%)
  local copies, waits for them, and re-layouts  108 us (17%)
  matrix products  87.6 us (14%)
  other arithmetic  45.5 us (7%)
  between operations  17 us (3%)
    psum x1, blocking collectives, shards(): lax.psum(grad_first_gain.astype(jnp.bfloat16), 'ep').astype(jnp.float32)  61.7 us
    reduce_scatter x2, waiting for transfers between devices, send_home(): lax.psum_scatter(blocks, 'tp', scatter_dimension=1, tiled=True)  58.6 us
    psum x1, waiting for transfers between devices, shards(): lax.psum(grad_query_weight.astype(jnp.bfloat16), 'ep').astype(jnp.float32)  40.5 us
    all_to_all x2, blocking collectives, send_home(): lax.all_to_all(shares, 'ep', split_axis=0, concat_axis=0, tiled=True)  37.5 us
    all_gather x2, waiting for transfers between devices, send_home(): lax.all_gather(moved, 'tp', axis=1, tiled=True).reshape(-1, model_width)  37.4 us
    all_to_all x2, blocking collectives, send_out(): moved = lax.all_to_all(piece, 'ep', split_axis=0, concat_axis=0, tiled=True)  35.6 us
    reduce_scatter x2, waiting for transfers between devices, total_of(): lax.psum_scatter(padded_to(lines, lax.axis_size(axis)), axis, scatter_dim...  33 us
    all_gather x2, waiting for transfers between devices, send_out(): lax.all_gather(moved, 'tp', axis=1, tiled=True).reshape(-1, model_width)  27 us
  transfers between devices with their start and end apart: 10, of which 8 were waited for; matrix products, arithmetic and copies ran while one was open for 21% of the time, Pallas kernels for 0%

commit v1 on v0

v1 whole, which is shorter than its diff:
```python
from functools import partial

import jax
import jax.numpy as jnp
from jax import lax
from jax.experimental import pallas as pl
from jax.experimental.pallas import tpu as pltpu
from jax.sharding import PartitionSpec as P

HEAD_SIZE = 64
EPS = 1e-05
THETA = 150000.0
LIMIT = 7.0
ALPHA = 1.702
NEGATIVE = -1e30

D = 2880
FF_LOCAL = 360
SHARE = 384
BLOCKS = 8
WIDE = SHARE * BLOCKS
ROWS = 128
EXPERTS = 16
CAP = 48
SLOTS = EXPERTS * CAP
HALF = SLOTS // 2
QUARTER = SLOTS // 4
MESH = pl.DeviceIdType.MESH
F32 = jnp.float32
BF16 = jnp.bfloat16
HIGHEST = lax.Precision.HIGHEST


def product(left, right):
    return jnp.dot(left, right, preferred_element_type=F32)


def contract_rows(left, right):
    return lax.dot_general(left, right, (((0,), (0,)), ((), ())), preferred_element_type=F32)


def against_rows(left, right):
    return lax.dot_general(left, right, (((1,), (1,)), ((), ())), preferred_element_type=F32)


def exact_against_rows(left, right):
    return lax.dot_general(
        left, right, (((1,), (1,)), ((), ())), preferred_element_type=F32, precision=HIGHEST
    )


def rms_norm(value_rows, gain_vector):
    return (
        value_rows
        * lax.rsqrt(jnp.mean(value_rows * value_rows, axis=-1, keepdims=True) + EPS)
        * gain_vector
    )


def angles_of(positions, head_width):
    exponent = jnp.arange(head_width // 2, dtype=F32) * (2.0 / head_width)
    frequency = jnp.power(THETA, -exponent)
    return positions.astype(F32)[:, None] * frequency[None, :]


def apply_rotary(value_rows, rotary_angles):
    half_width = value_rows.shape[-1] // 2
    cosine = jnp.cos(rotary_angles)[:, None, :]
    sine_part = jnp.sin(rotary_angles)[:, None, :]
    first_half = value_rows[..., :half_width]
    second_half = value_rows[..., half_width:]
    return jnp.concatenate(
        [
            first_half * cosine - second_half * sine_part,
            second_half * cosine + first_half * sine_part,
        ],
        axis=-1,
    )


def layout(lengths_row, count_of_rows):
    row_index = jnp.arange(count_of_rows, dtype=jnp.int32)
    first_end = lengths_row[0]
    second_end = lengths_row[0] + lengths_row[1]
    document = (row_index >= first_end).astype(jnp.int32) + (row_index >= second_end).astype(
        jnp.int32
    )
    doc_start = jnp.where(document == 0, 0, jnp.where(document == 1, first_end, second_end))
    return (row_index - doc_start, document)


def log_totals(scores, sink_logit_column):
    highest = jnp.maximum(jnp.max(scores, axis=-1), sink_logit_column)
    total = jnp.exp(sink_logit_column - highest) + jnp.sum(
        jnp.exp(scores - highest[..., None]), axis=-1
    )
    return highest + jnp.log(total)


class Place:
    def __init__(self):
        self.ep = lax.axis_index("ep")
        self.tp = lax.axis_index("tp")
        self.z, self.x = self.ep // 4, self.ep % 4
        self.y, self.core = self.tp // 2, self.tp % 2

    def sibling(self):
        return (self.ep, self.y * 2 + (1 - self.core))

    def along_y(self, step):
        return (self.ep, lax.rem(self.y + step, 4) * 2 + self.core)

    def along_tp(self, step):
        return (self.ep, lax.rem(self.tp + step, 8))

    def along_ep(self, k):
        z = lax.rem(self.z + k // 4, 4)
        x = lax.rem(self.x + k % 4, 4)
        return (z * 4 + x, self.tp)

    def back_ep(self, k):
        z = lax.rem(self.z + 4 - k // 4, 4)
        x = lax.rem(self.x + 4 - k % 4, 4)
        return (z * 4 + x, self.tp)


class Sender:
    def __init__(self, send_sems, recv_sems):
        self.send_sems, self.recv_sems = send_sems, recv_sems
        self.used = 0
        self.open = []

    def start(self, source, target, device):
        n = self.used
        self.used += 1
        copy = pltpu.make_async_remote_copy(
            src_ref=source,
            dst_ref=target,
            send_sem=self.send_sems.at[n],
            recv_sem=self.recv_sems.at[n],
            device_id=device,
            device_id_type=MESH,
        )
        copy.start()
        self.open.append(copy)
        return n

    def arrived(self, n, target):
        pltpu.make_async_remote_copy(
            src_ref=target,
            dst_ref=target,
            send_sem=self.send_sems.at[n],
            recv_sem=self.recv_sems.at[n],
            device_id=Place().sibling(),
            device_id_type=MESH,
        ).wait_recv()

    def finish(self):
        for copy in self.open:
            copy.wait_send()
        self.open = []


def column_of(row):
    return jnp.transpose(jnp.broadcast_to(row, (128, 128)))


def wide(columns, width=SHARE):
    return jnp.concatenate([columns] * (width // 128), axis=1)


def share_blocks(part, emit):
    for q in range(BLOCKS):
        lo = q * SHARE
        width = min(SHARE, D - lo)
        block = part(lo, width)
        if width < SHARE:
            block = jnp.concatenate(
                [block, jnp.zeros((block.shape[0], SHARE - width), block.dtype)], axis=1
            )
        emit(q, block)


def reduce_columns(me, send, part, from_sibling, sums, from_y):
    order = (2, 1, 3, 0)
    ticket = []
    for i, step in enumerate(order):
        y = lax.rem(me.y + step, 4)
        ticket.append(
            send.start(part.at[y * 2 + 1 - me.core], from_sibling.at[i], me.sibling())
        )
    landed = []
    for i, step in enumerate(order):
        y = lax.rem(me.y + step, 4)
        send.arrived(ticket[i], from_sibling.at[i])
        total = part[y * 2 + me.core].astype(F32) + from_sibling[i].astype(F32)
        if step:
            sums[i] = total.astype(BF16)
            landed.append(send.start(sums.at[i], from_y.at[i], me.along_y(step)))
    for i, n in enumerate(landed):
        send.arrived(n, from_y.at[i])
        total = total + from_y[i].astype(F32)
    return total


def exchange(me, send, own, others):
    tickets = [send.start(own, others.at[i - 1], me.along_tp(i)) for i in range(1, 8)]
    total = own[...]
    for i, n in enumerate(tickets):
        send.arrived(n, others.at[i])
        total = total + others[i]
    return total


def gather_columns(me, send, blocks):
    own = blocks.at[me.tp]
    to_y = [send.start(own, own, me.along_y(step)) for step in (2, 1, 3)]
    to_sibling = [send.start(own, own, me.sibling())]
    for n, step in zip(to_y, (2, 1, 3)):
        block = blocks.at[lax.rem(me.y + 4 - step, 4) * 2 + me.core]
        send.arrived(n, block)
        to_sibling.append(send.start(block, block, me.sibling()))
    for n, step in zip(to_sibling, (0, 2, 1, 3)):
        send.arrived(n, blocks.at[lax.rem(me.y + 4 - step, 4) * 2 + 1 - me.core])


def greet_tp(me):
    barrier = pltpu.get_barrier_semaphore()
    for i in range(1, 8):
        pl.semaphore_signal(barrier, inc=1, device_id=me.along_tp(i), device_id_type=MESH)
    return lambda: pl.semaphore_wait(barrier, 7)


def greet_all(me):
    barrier = pltpu.get_barrier_semaphore()
    for i in range(1, 8):
        pl.semaphore_signal(barrier, inc=1, device_id=me.along_tp(i), device_id_type=MESH)
    for k in range(1, 16):
        pl.semaphore_signal(barrier, inc=1, device_id=me.along_ep(k), device_id_type=MESH)
    return lambda: pl.semaphore_wait(barrier, 22)


def attend_kernel(
    heads, weight, inputs, vectors, router, router_bias, chosen,
    second, mixed_out, stat_out,
    part, from_sibling, sums, from_y, stat, stats, send_sems, recv_sems,
):
    me = Place()
    send = Sender(send_sems, recv_sems)
    all_here = greet_tp(me)
    rows = heads[...]

    def emit(q, block):
        part[q] = block.astype(BF16)

    share_blocks(lambda lo, width: product(rows, weight[:, lo : lo + width]), emit)
    all_here()
    attended = reduce_columns(me, send, part, from_sibling, sums, from_y)
    mixed = inputs[...] + attended + vectors[0:1, :]
    mixed_out[...] = mixed
    raised = mixed * vectors[1:2, :]
    stat[0:16, :] = against_rows(router[...], raised.astype(BF16))
    stat[16:24, :] = exact_against_rows(jnp.ones((8, SHARE), F32), mixed * mixed)
    total = exchange(me, send, stat, stats)
    scale = lax.rsqrt(total[16:17, :] * (1.0 / D) + EPS)
    second[...] = (raised * wide(column_of(scale))).astype(BF16)
    plain = total[0:16, :] * scale
    logits = plain + router_bias[...]
    taken = chosen[...] > 0.5
    highest = jnp.max(jnp.where(taken, logits, NEGATIVE), axis=0, keepdims=True)
    lifted = jnp.where(taken, jnp.exp(jnp.where(taken, logits, highest) - highest), 0.0)
    stat_out[0:16, :] = lifted / jnp.sum(lifted, axis=0, keepdims=True)
    stat_out[16:32, :] = plain
    stat_out[32:40, :] = jnp.broadcast_to(scale, (8, 128))
    send.finish()


def attend_end(heads, weight, inputs, vectors, router, router_bias, chosen):
    return pl.pallas_call(
        attend_kernel,
        out_shape=(
            jax.ShapeDtypeStruct((ROWS, SHARE), BF16),
            jax.ShapeDtypeStruct((ROWS, SHARE), F32),
            jax.ShapeDtypeStruct((40, 128), F32),
        ),
        in_specs=[pl.BlockSpec(memory_space=pltpu.VMEM)] * 7,
        out_specs=(pl.BlockSpec(memory_space=pltpu.VMEM),) * 3,
        scratch_shapes=[
            pltpu.VMEM((8, ROWS, SHARE), BF16),
            pltpu.VMEM((4, ROWS, SHARE), BF16),
            pltpu.VMEM((3, ROWS, SHARE), BF16),
            pltpu.VMEM((3, ROWS, SHARE), BF16),
            pltpu.VMEM((24, 128), F32),
            pltpu.VMEM((7, 24, 128), F32),
            pltpu.SemaphoreType.DMA((14,)),
            pltpu.SemaphoreType.DMA((14,)),
        ],
        compiler_params=pltpu.CompilerParams(
            collective_id=1, has_side_effects=True, vmem_limit_bytes=40 * 2**20
        ),
        name="attend_end",
    )(heads, weight, inputs, vectors, router, router_bias, chosen)


def activation_parts(gate_pre, up_pre):
    lowered = LIMIT - gate_pre
    cap = jnp.maximum(lowered, 0.0) + jnp.log(1.0 + jnp.exp(-jnp.abs(lowered)))
    capped_gate = LIMIT - cap
    tanh = jnp.tanh(up_pre * (1.0 / LIMIT))
    capped_up = LIMIT * tanh
    sigmoid = 1.0 / (1.0 + jnp.exp(-ALPHA * capped_gate))
    return lowered, capped_gate, tanh, capped_up, sigmoid


def expert_kernel(
    second, mixed, stat, selector, selector_t, cotangent, cot_own, gateup, down, gateup_bias, down_bias,
    router, vectors,
    rows_out, cots_out, scaled_out, grad_gate_out, grad_up_out, gate_cols_out,
    grad_att_out, layer_out, small_out, bias_out,
    R, C, weights, staged, staged_c, gates_send, gates, gate_pre, up_pre, hidden,
    to_sibling, kept, from_sibling, sums, results, from_y, home, wire, from_y_small, stat_own, stats,
    both, send_sems, recv_sems, local_sems,
):
    me = Place()
    send = Sender(send_sems, recv_sems)
    all_here = greet_all(me)
    load = pltpu.make_async_copy(gateup, weights.at[:, 0:D, :], local_sems.at[0])
    load.start()
    weights[:, D:, :] = jnp.zeros((2, WIDE - D, FF_LOCAL), BF16)
    staged[...] = product(selector[...], second[...]).astype(BF16)
    staged_c[...] = product(selector[...], cot_own[...]).astype(BF16)
    for k in range(EXPERTS):
        row = jnp.broadcast_to(stat[k : k + 1, :], (8, 128))
        picked = exact_against_rows(row, selector[k * CAP : (k + 1) * CAP, :].astype(F32))
        gates_send[k] = jnp.concatenate([picked, jnp.zeros((8, 128 - CAP), F32)], axis=1)
    all_here()

    def scatter(source, target):
        tickets = [None]
        for k in range(1, EXPERTS):
            lines = pl.ds(k * CAP, CAP)
            tickets.append(
                send.start(source.at[lines], target.at[me.tp, lines], me.along_ep(k))
            )
        target[me.tp, 0:CAP, :] = source[0:CAP, :]
        return tickets

    rows_in = scatter(staged, R)
    gates_in = [None]
    for k in range(1, EXPERTS):
        gates_in.append(send.start(gates_send.at[k], gates.at[k], me.along_ep(k)))
    gates[0] = gates_send[0]
    cots_in = scatter(staged_c, C)

    steps = (1, 3, 2)

    def spread(buffer, tickets, j):
        lines = pl.ds(j * QUARTER, QUARTER)
        for k in range(4 * j, 4 * j + 4):
            if k:
                send.arrived(tickets[k], buffer.at[me.tp, pl.ds(k * CAP, CAP)])
        own = buffer.at[me.tp, lines]
        return [send.start(own, own, me.along_y(s)) for s in steps] + [
            send.start(own, own, me.sibling())
        ]

    def pass_on(buffer, tickets, j):
        lines = pl.ds(j * QUARTER, QUARTER)
        sent = [tickets[3]]
        for n, s in zip(tickets, steps):
            block = buffer.at[lax.rem(me.y + 4 - s, 4) * 2 + me.core, lines]
            send.arrived(n, block)
            sent.append(send.start(block, block, me.sibling()))
        return sent

    def complete(buffer, tickets, j):
        lines = pl.ds(j * QUARTER, QUARTER)
        for n, s in zip(tickets, (0,) + steps):
            send.arrived(n, buffer.at[lax.rem(me.y + 4 - s, 4) * 2 + 1 - me.core, lines])

    a, b = [None] * 4, [None] * 4
    a[0] = spread(R, rows_in, 0)
    a[1] = spread(R, rows_in, 1)
    a[0] = pass_on(R, a[0], 0)
    a[2] = spread(R, rows_in, 2)
    a[1] = pass_on(R, a[1], 1)
    a[3] = spread(R, rows_in, 3)
    a[2] = pass_on(R, a[2], 2)
    for j in range(4):
        b[j] = spread(C, cots_in, j)
    complete(R, a[0], 0)
    complete(R, a[1], 1)
    load.wait()

    def lines_of(h):
        return pl.ds(h * HALF, HALF)

    def forward(h):
        lines = lines_of(h)
        gate_pre[lines, :] = jnp.broadcast_to(gateup_bias[0:1, :], (HALF, FF_LOCAL))
        up_pre[lines, :] = jnp.broadcast_to(gateup_bias[1:2, :], (HALF, FF_LOCAL))

        @pl.loop(0, 4)
        def _(y):
            block = jnp.concatenate([R[2 * y, lines, :], R[2 * y + 1, lines, :]], axis=1)
            span = pl.ds(pl.multiple_of(y * 2 * SHARE, 2 * SHARE), 2 * SHARE)
            gate_pre[lines, :] += product(block, weights[0, span, :])
            up_pre[lines, :] += product(block, weights[1, span, :])

        _, capped_gate, _, capped_up, sigmoid = activation_parts(
            gate_pre[lines, :], up_pre[lines, :]
        )
        hidden[lines, :] = ((capped_up + 1.0) * capped_gate * sigmoid).astype(BF16)

        def out_block(q):
            span = pl.ds(pl.multiple_of(q * SHARE, SHARE), SHARE)
            return product(hidden[lines, :], down[:, span]) + down_bias[pl.ds(q, 1), :]

        sent = []
        for y in range(4):
            to_sibling[0, y, lines, :] = out_block(2 * y + 1 - me.core).astype(BF16)
            sent.append(
                send.start(
                    to_sibling.at[0, y, lines], from_sibling.at[0, y, lines], me.sibling()
                )
            )
        for y in range(4):
            kept[0, y, lines, :] = out_block(2 * y + me.core).astype(BF16)
        return sent

    def results_home(h, sent):
        lines = lines_of(h)
        for y in range(4):
            send.arrived(sent[y], from_sibling.at[0, y, lines])
            sums[0, y, lines, :] = (
                kept[0, y, lines, :].astype(F32) + from_sibling[0, y, lines, :].astype(F32)
            ).astype(BF16)
        tickets = []
        for k in range(8 * h, 8 * h + 8):
            span = pl.ds(k * CAP, CAP)
            if k:
                tickets.append(
                    send.start(sums.at[0, :, span], results.at[:, span], me.back_ep(k))
                )
            else:
                tickets.append(None)
                results[:, 0:CAP, :] = sums[0, :, 0:CAP, :]
        return tickets

    sent_0 = forward(0)
    a[3] = pass_on(R, a[3], 3)
    b[0] = pass_on(C, b[0], 0)
    complete(R, a[2], 2)
    complete(R, a[3], 3)
    rows_copy = pltpu.make_async_copy(R, rows_out, local_sems.at[1])
    rows_copy.start()
    sent_1 = forward(1)
    back = results_home(0, sent_0)
    for j in (1, 2, 3):
        b[j] = pass_on(C, b[j], j)
    back = back + results_home(1, sent_1)
    for k in range(1, EXPERTS):
        send.arrived(gates_in[k], gates.at[k])
    gate_rows = jnp.concatenate(
        [gates[:, 0, :], jnp.zeros((128 - EXPERTS, 128), F32)], axis=0
    )
    gate_cols = jnp.transpose(gate_rows)

    def gate_column(h):
        return jnp.concatenate(
            [gate_cols[0:CAP, k : k + 1] for k in range(8 * h, 8 * h + 8)], axis=0
        )

    def backward(h):
        lines = lines_of(h)
        gate = gate_column(h)
        high = gate.astype(BF16)
        low = (gate - high.astype(F32)).astype(BF16)
        place = lax.broadcasted_iota(jnp.int32, (HALF, 128), 1)
        gate_cols_out[lines, :] = jnp.where(
            place == 0,
            high.astype(F32),
            jnp.where(place == 1, low.astype(F32), 0.0),
        ).astype(BF16)

        def step(y, total):
            block = jnp.concatenate([C[2 * y, lines, :], C[2 * y + 1, lines, :]], axis=1)
            span = pl.ds(pl.multiple_of(y * 2 * SHARE, 2 * SHARE), 2 * SHARE)
            return total + against_rows(block, down[:, span])

        grad_hidden = gate * lax.fori_loop(0, 4, step, jnp.zeros((HALF, FF_LOCAL), F32))
        lowered, capped_gate, tanh, capped_up, sigmoid = activation_parts(
            gate_pre[lines, :], up_pre[lines, :]
        )
        scaled_out[lines, :] = (gate * hidden[lines, :].astype(F32)).astype(BF16)
        slope = (capped_up + 1.0) * (
            sigmoid + ALPHA * capped_gate * sigmoid * (1.0 - sigmoid)
        )
        grad_gate_out[lines, :] = (
            grad_hidden * slope * (1.0 / (1.0 + jnp.exp(-lowered)))
        ).astype(BF16)
        grad_up_out[lines, :] = (
            grad_hidden * capped_gate * sigmoid * (1.0 - tanh * tanh)
        ).astype(BF16)

        def back_block(q):
            span = pl.ds(pl.multiple_of(q * SHARE, SHARE), SHARE)
            return against_rows(grad_gate_out[lines, :], weights[0, span, :]) + against_rows(
                grad_up_out[lines, :], weights[1, span, :]
            )

        sent = []
        for s in (2, 1, 3, 0):
            y = lax.rem(me.y + s, 4)
            to_sibling[1, s, lines, :] = back_block(2 * y + 1 - me.core).astype(BF16)
            sent.append(
                send.start(
                    to_sibling.at[1, s, lines], from_sibling.at[1, s, lines], me.sibling()
                )
            )
        landed = []
        for s, n in zip((2, 1, 3, 0), sent):
            y = lax.rem(me.y + s, 4)
            block = back_block(2 * y + me.core)
            send.arrived(n, from_sibling.at[1, s, lines])
            total = block + from_sibling[1, s, lines, :].astype(F32)
            if s:
                sums[1, s, lines, :] = total.astype(BF16)
                landed.append(
                    send.start(
                        sums.at[1, s, lines], from_y.at[s - 1, lines], me.along_y(s)
                    )
                )
            else:
                kept[1, 0, lines, :] = total.astype(BF16)
        return landed

    def grads_home(h, landed):
        lines = lines_of(h)
        total = kept[1, 0, lines, :].astype(F32)
        for s, n in zip((2, 1, 3), landed):
            send.arrived(n, from_y.at[s - 1, lines])
            total = total + from_y[s - 1, lines, :].astype(F32)
        sums[1, 0, lines, :] = total.astype(BF16)
        tickets = []
        for k in range(8 * h, 8 * h + 8):
            span = pl.ds(k * CAP, CAP)
            if k:
                tickets.append(
                    send.start(sums.at[1, 0, span], home.at[span], me.back_ep(k))
                )
            else:
                tickets.append(None)
                home[0:CAP, :] = sums[1, 0, 0:CAP, :]
        return tickets

    complete(C, b[0], 0)
    complete(C, b[1], 1)
    landed_0 = backward(0)
    complete(C, b[2], 2)
    complete(C, b[3], 3)
    cots_copy = pltpu.make_async_copy(C, cots_out, local_sems.at[2])
    cots_copy.start()
    landed_1 = backward(1)
    home_in = grads_home(0, landed_0)
    home_in = home_in + grads_home(1, landed_1)

    for k in range(1, EXPERTS):
        send.arrived(back[k], results.at[:, pl.ds(k * CAP, CAP)])
    spread_gates = jnp.concatenate(
        [jnp.broadcast_to(stat[k : k + 1, :], (CAP, 128)) for k in range(EXPERTS)], axis=0
    )
    weighted = selector[...].astype(F32) * spread_gates
    high = weighted.astype(BF16)
    low = (weighted - high.astype(F32)).astype(BF16)
    pairs = jnp.zeros((SLOTS, ROWS), F32)
    to_y = []
    for s in (2, 1, 3, 0):
        y = lax.rem(me.y + s, 4)
        block = results[y]
        pairs = pairs + against_rows(block, cotangent[2 * y + me.core])
        mine = contract_rows(high, block) + contract_rows(low, block)
        if s:
            wire[s - 1] = mine.astype(BF16)
            to_y.append(send.start(wire.at[s - 1], from_y_small.at[s - 1], me.along_y(s)))
    pairs = pairs * selector[...].astype(F32)
    for k in range(EXPERTS):
        stat_own[k : k + 1, :] = jnp.sum(pairs[k * CAP : (k + 1) * CAP], axis=0, keepdims=True)
    for k in range(1, EXPERTS):
        send.arrived(home_in[k], home.at[pl.ds(k * CAP, CAP)])
    returned = product(selector_t[...], home[...])
    gain = vectors[1:2, :]
    scale = wide(column_of(stat[32:33, :]))
    normal = mixed[...] * scale
    stat_own[16:24, :] = exact_against_rows(
        jnp.ones((8, SHARE), F32), returned * gain * normal
    )
    total = exchange(me, send, stat_own, stats)
    gate_share = stat[0:16, :]
    grad_gates = total[0:16, :]
    grad_logits = gate_share * (
        grad_gates - jnp.sum(gate_share * grad_gates, axis=0, keepdims=True)
    )
    inner = total[16:17, :] + jnp.sum(grad_logits * stat[16:32, :], axis=0, keepdims=True)
    grad_second = returned + lax.dot_general(
        grad_logits,
        router[...].astype(F32),
        (((0,), (0,)), ((), ())),
        preferred_element_type=F32,
        precision=HIGHEST,
    )
    final = cot_own[...].astype(F32)
    grad_mixed = final + scale * (
        gain * grad_second - normal * wide(column_of(inner * (1.0 / D)))
    )
    grad_att = grad_mixed.astype(BF16)
    for s, n in zip((2, 1, 3), to_y):
        send.arrived(n, from_y_small.at[s - 1])
        mine = mine + from_y_small[s - 1].astype(F32)
    both[me.tp, 0:ROWS, :] = grad_att
    both[me.tp, ROWS:, :] = (mixed[...] + mine).astype(BF16)
    small_out[0:16, :] = lax.dot_general(
        grad_logits,
        second[...].astype(F32),
        (((1,), (0,)), ((), ())),
        preferred_element_type=F32,
        precision=HIGHEST,
    )
    small_out[16:17, :] = jnp.sum(grad_second * normal, axis=0, keepdims=True)
    small_out[17:18, :] = jnp.sum(grad_att.astype(F32), axis=0, keepdims=True)
    small_out[18:24, :] = jnp.zeros((6, SHARE), F32)
    bias_out[...] = grad_logits
    gather_columns(me, send, both)
    grad_att_out[...] = both[:, 0:ROWS, :]
    layer_out[...] = both[:, ROWS:, :]
    rows_copy.wait()
    cots_copy.wait()
    send.finish()


def experts(*operands):
    vmem = pl.BlockSpec(memory_space=pltpu.VMEM)
    hbm = pl.BlockSpec(memory_space=pl.ANY)
    shape = jax.ShapeDtypeStruct
    count = 256
    return pl.pallas_call(
        expert_kernel,
        out_shape=(
            shape((8, SLOTS, SHARE), BF16),
            shape((8, SLOTS, SHARE), BF16),
            shape((SLOTS, FF_LOCAL), BF16),
            shape((SLOTS, FF_LOCAL), BF16),
            shape((SLOTS, FF_LOCAL), BF16),
            shape((SLOTS, 128), BF16),
            shape((8, ROWS, SHARE), BF16),
            shape((8, ROWS, SHARE), BF16),
            shape((24, SHARE), F32),
            shape((16, 128), F32),
        ),
        in_specs=[vmem] * 7 + [hbm] + [vmem] * 5,
        out_specs=(hbm, hbm) + (vmem,) * 8,
        scratch_shapes=[
            pltpu.VMEM((8, SLOTS, SHARE), BF16),
            pltpu.VMEM((8, SLOTS, SHARE), BF16),
            pltpu.VMEM((2, WIDE, FF_LOCAL), BF16),
            pltpu.VMEM((SLOTS, SHARE), BF16),
            pltpu.VMEM((SLOTS, SHARE), BF16),
            pltpu.VMEM((EXPERTS, 8, 128), F32),
            pltpu.VMEM((EXPERTS, 8, 128), F32),
            pltpu.VMEM((SLOTS, FF_LOCAL), F32),
            pltpu.VMEM((SLOTS, FF_LOCAL), F32),
            pltpu.VMEM((SLOTS, FF_LOCAL), BF16),
            pltpu.VMEM((2, 4, SLOTS, SHARE), BF16),
            pltpu.VMEM((2, 4, SLOTS, SHARE), BF16),
            pltpu.VMEM((2, 4, SLOTS, SHARE), BF16),
            pltpu.VMEM((2, 4, SLOTS, SHARE), BF16),
            pltpu.VMEM((4, SLOTS, SHARE), BF16),
            pltpu.VMEM((3, SLOTS, SHARE), BF16),
            pltpu.VMEM((SLOTS, SHARE), BF16),
            pltpu.VMEM((3, ROWS, SHARE), BF16),
            pltpu.VMEM((3, ROWS, SHARE), BF16),
            pltpu.VMEM((24, 128), F32),
            pltpu.VMEM((7, 24, 128), F32),
            pltpu.VMEM((8, 2 * ROWS, SHARE), BF16),
            pltpu.SemaphoreType.DMA((count,)),
            pltpu.SemaphoreType.DMA((count,)),
            pltpu.SemaphoreType.DMA((3,)),
        ],
        compiler_params=pltpu.CompilerParams(
            collective_id=2, has_side_effects=True, vmem_limit_bytes=60 * 2**20
        ),
        name="experts",
    )(*operands)


def expert_grads_kernel(rows, cots, scaled, grad_gate, grad_up, gate_cols, gateup, down, bias):
    gateup[0] = contract_rows(rows[0], grad_gate[...])
    gateup[1] = contract_rows(rows[0], grad_up[...])
    down[...] = contract_rows(scaled[...], cots[0])
    bias[0] = contract_rows(gate_cols[...], cots[0])[0:8]


def expert_grads(rows, cots, scaled, grad_gate, grad_up, gate_cols):
    whole = pl.BlockSpec((SLOTS, FF_LOCAL), lambda p: (0, 0))
    block = pl.BlockSpec((1, SLOTS, SHARE), lambda p: (p, 0, 0))
    shape = jax.ShapeDtypeStruct
    return pl.pallas_call(
        expert_grads_kernel,
        grid=(BLOCKS,),
        out_shape=(
            shape((2, D, FF_LOCAL), F32),
            shape((FF_LOCAL, D), F32),
            shape((BLOCKS, 8, SHARE), F32),
        ),
        in_specs=[block, block, whole, whole, whole, pl.BlockSpec((SLOTS, 128), lambda p: (0, 0))],
        out_specs=(
            pl.BlockSpec((2, SHARE, FF_LOCAL), lambda p: (0, p, 0)),
            pl.BlockSpec((FF_LOCAL, SHARE), lambda p: (0, p)),
            pl.BlockSpec((1, 8, SHARE), lambda p: (p, 0, 0)),
        ),
        compiler_params=pltpu.CompilerParams(vmem_limit_bytes=40 * 2**20),
        cost_estimate=pl.CostEstimate(
            flops=6 * SLOTS * D * FF_LOCAL, bytes_accessed=22_000_000, transcendentals=0
        ),
        name="expert_grads",
    )(rows, cots, scaled, grad_gate, grad_up, gate_cols)


def input_kernel(
    grad_query, grad_key, grad_value, query_weight, key_weight, value_weight, inputs, scale_row,
    vectors, grad_mixed,
    tokens_out, small_out,
    part, from_sibling, sums, from_y, stat, stats, blocks, send_sems, recv_sems,
):
    me = Place()
    send = Sender(send_sems, recv_sems)
    all_here = greet_tp(me)

    def grad(lo, width):
        return (
            against_rows(grad_query[...], query_weight[lo : lo + width, :])
            + against_rows(grad_key[...], key_weight[lo : lo + width, :])
            + against_rows(grad_value[...], value_weight[lo : lo + width, :])
        )

    def emit(q, block):
        part[q] = block.astype(BF16)

    share_blocks(grad, emit)
    all_here()
    grad_normed = reduce_columns(me, send, part, from_sibling, sums, from_y)
    scale = wide(column_of(scale_row[0:1, :]))
    normal = inputs[...] * scale
    raised = vectors[2:3, :] * grad_normed
    stat[...] = exact_against_rows(jnp.ones((8, SHARE), F32), raised * normal)
    total = exchange(me, send, stat, stats)
    tokens = grad_mixed[me.tp].astype(F32) + scale * (
        raised - normal * wide(column_of(total[0:1, :] * (1.0 / D)))
    )
    blocks[me.tp] = tokens.astype(BF16)
    small_out[...] = jnp.broadcast_to(
        jnp.sum(grad_normed * normal, axis=0, keepdims=True), (8, SHARE)
    )
    gather_columns(me, send, blocks)
    tokens_out[...] = blocks[...]
    send.finish()


def input_grad(*operands):
    return pl.pallas_call(
        input_kernel,
        out_shape=(
            jax.ShapeDtypeStruct((8, ROWS, SHARE), BF16),
            jax.ShapeDtypeStruct((8, SHARE), F32),
        ),
        in_specs=[pl.BlockSpec(memory_space=pltpu.VMEM)] * 10,
        out_specs=(pl.BlockSpec(memory_space=pltpu.VMEM),) * 2,
        scratch_shapes=[
            pltpu.VMEM((8, ROWS, SHARE), BF16),
            pltpu.VMEM((4, ROWS, SHARE), BF16),
            pltpu.VMEM((3, ROWS, SHARE), BF16),
            pltpu.VMEM((3, ROWS, SHARE), BF16),
            pltpu.VMEM((8, 128), F32),
            pltpu.VMEM((7, 8, 128), F32),
            pltpu.VMEM((8, ROWS, SHARE), BF16),
            pltpu.SemaphoreType.DMA((21,)),
            pltpu.SemaphoreType.DMA((21,)),
        ],
        compiler_params=pltpu.CompilerParams(
            collective_id=3, has_side_effects=True, vmem_limit_bytes=40 * 2**20
        ),
        name="input_grad",
    )(*operands)


def joined(blocks):
    return jnp.concatenate([blocks[q] for q in range(BLOCKS)], axis=1)[:, :D]


def shards(
    tokens,
    seq_lengths,
    expert_ids,
    first_gain,
    query_weight,
    key_matrix,
    value_matrix,
    query_bias,
    key_offset_bias,
    value_offset_bias,
    head_sink_logits,
    output_weight,
    output_bias,
    second_gain,
    router_weight,
    router_bias,
    expert_gateup,
    gateup_bias,
    expert_down,
    down_bias,
    cotangent,
):
    tp_place = lax.axis_index("tp")
    ep_place = lax.axis_index("ep")
    place_z, place_x = ep_place // 4, ep_place % 4
    heads_local = query_weight.shape[1] // HEAD_SIZE
    score_scale = HEAD_SIZE ** (-0.5)

    def own_columns(array):
        padded = jnp.pad(array, ((0, 0), (0, WIDE - D)))
        return lax.dynamic_slice_in_dim(padded, tp_place * SHARE, SHARE, 1)

    distance = jnp.arange(EXPERTS)
    expert_of = ((place_z + distance // 4) % 4) * 4 + (place_x + distance % 4) % 4
    turn = (expert_of[:, None] == jnp.arange(EXPERTS)[None, :]).astype(F32)
    chosen = jnp.sum(
        (expert_ids.T[:, None, :] == expert_of[None, :, None]).astype(F32), axis=0
    )
    earlier = (jnp.arange(ROWS)[:, None] < jnp.arange(ROWS)[None, :]).astype(BF16)
    rank = product(chosen.astype(BF16), earlier).astype(jnp.int32)
    at_slot = (rank[:, None, :] == jnp.arange(CAP)[None, :, None]) & (chosen[:, None, :] > 0.5)
    selector = at_slot.astype(BF16).reshape(SLOTS, ROWS)
    selector_t = selector.T
    vectors = own_columns(
        jnp.concatenate(
            [
                output_bias[None],
                second_gain[None],
                first_gain[None],
                jnp.zeros((5, D), F32),
            ]
        )
    )
    router_t = own_columns(product(turn.astype(BF16), router_weight.T).astype(BF16))
    router_bias_turned = jnp.broadcast_to(
        jnp.sum(turn * router_bias[None, :], axis=1, keepdims=True), (EXPERTS, ROWS)
    )
    cot_blocks = jnp.pad(cotangent, ((0, 0), (0, WIDE - D))).reshape(ROWS, BLOCKS, SHARE)
    cot_blocks = cot_blocks.transpose(1, 0, 2)
    cot_own = own_columns(cotangent)
    down = jnp.pad(expert_down[0], ((0, 0), (0, WIDE - D)))
    first_slice = jnp.where(tp_place == 0, 1.0, 0.0).astype(F32)
    down_bias_blocks = jnp.pad(first_slice * down_bias[0], (0, WIDE - D)).reshape(BLOCKS, SHARE)
    gateup_bias_local = jnp.pad(gateup_bias[0], ((0, 6), (0, 0)))

    lengths_row = lax.dynamic_index_in_dim(seq_lengths, ep_place, 0, keepdims=False)
    positions, document = layout(lengths_row, ROWS)
    rotary_angles = angles_of(positions, HEAD_SIZE)
    row_index = jnp.arange(ROWS)
    allowed = (document[:, None] == document[None, :]) & (row_index[None, :] <= row_index[:, None])
    sink_logit_column = head_sink_logits[:, None]
    inputs = tokens.astype(F32)
    first_scale = lax.rsqrt(jnp.mean(inputs * inputs, axis=-1) + EPS)
    normed_low = (inputs * first_scale[:, None] * first_gain).astype(BF16)
    all_normed = lax.all_gather(normed_low, "ep", axis=0, tiled=True)
    query_unrotated = product(normed_low, query_weight) + query_bias
    key_unrotated = product(normed_low, key_matrix) + key_offset_bias
    value_low = (product(normed_low, value_matrix) + value_offset_bias).astype(BF16)

    def rotate_both(query_in, key_in):
        return (
            apply_rotary(query_in.reshape(ROWS, heads_local, HEAD_SIZE), rotary_angles),
            apply_rotary(key_in.reshape(ROWS, 1, HEAD_SIZE), rotary_angles),
        )

    rotated, rotate_back = jax.vjp(rotate_both, query_unrotated, key_unrotated)
    query_low = rotated[0].astype(BF16)
    key_low = rotated[1].astype(BF16)[:, 0]

    def masked_scores():
        raw_scores = (
            jnp.einsum("qgd,kd->gqk", query_low, key_low, preferred_element_type=F32) * score_scale
        )
        return jnp.where(allowed[None], raw_scores, NEGATIVE)

    scores = masked_scores()
    log_total = log_totals(scores, sink_logit_column)
    probs_low = jnp.exp(scores - log_total[..., None]).astype(BF16)
    head_values = jnp.einsum("gqk,kd->qgd", probs_low, value_low, preferred_element_type=F32)
    heads_low = head_values.reshape(ROWS, heads_local * HEAD_SIZE).astype(BF16)
    all_heads = lax.all_gather(heads_low, "ep", axis=0, tiled=True)

    second, mixed, stat = attend_end(
        heads_low,
        output_weight,
        own_columns(inputs),
        vectors,
        router_t,
        router_bias_turned,
        chosen,
    )
    (
        expert_rows, cot_rows, scaled_hidden, grad_gate, grad_up, gate_cols,
        grad_att_blocks, layer_blocks, small, grad_logits,
    ) = experts(
        second, mixed, stat, selector, selector_t, cot_blocks, cot_own, expert_gateup[0], down,
        gateup_bias_local, down_bias_blocks, router_t, vectors,
    )
    grad_gateup, grad_down, grad_down_bias = expert_grads(
        expert_rows, cot_rows, scaled_hidden, grad_gate, grad_up, gate_cols
    )
    grad_gateup_bias = jnp.stack(
        [jnp.sum(grad_gate.astype(F32), axis=0), jnp.sum(grad_up.astype(F32), axis=0)]
    )[None]
    grad_down_bias = (grad_down_bias[:, 0] + grad_down_bias[:, 1]).reshape(1, WIDE)[:, :D]
    layer_output = joined(layer_blocks)
    grad_attended = joined(grad_att_blocks)
    all_grad_attended = lax.all_gather(grad_attended, "ep", axis=0, tiled=True)
    grad_output_weight = contract_rows(all_heads, all_grad_attended)

    grad_heads = (
        against_rows(grad_attended, output_weight).astype(BF16).reshape(ROWS, heads_local, HEAD_SIZE)
    )
    probs_full = jnp.exp(masked_scores() - log_total[..., None])
    grad_probs = jnp.einsum("qgd,kd->gqk", grad_heads, value_low, preferred_element_type=F32)
    row_delta = jnp.sum(probs_full * grad_probs, axis=-1)
    grad_scores = (probs_full * (grad_probs - row_delta[..., None])).astype(BF16)
    grad_sinks = -jnp.sum(jnp.exp(sink_logit_column - log_total) * row_delta, axis=-1)
    grad_values_low = jnp.einsum(
        "gqk,qgd->kd", probs_low, grad_heads, preferred_element_type=F32
    ).astype(BF16)
    grad_query_rot = (
        jnp.einsum("gqk,kd->qgd", grad_scores, key_low, preferred_element_type=F32) * score_scale
    )
    grad_key_rot = (
        jnp.einsum("gqk,qgd->kd", grad_scores, query_low, preferred_element_type=F32) * score_scale
    )
    grad_query_pre, grad_key_pre = rotate_back((grad_query_rot, grad_key_rot[:, None, :]))
    grad_query_low = grad_query_pre.astype(BF16)
    grad_key_low = grad_key_pre.astype(BF16)
    grad_heads_all = jnp.concatenate([grad_query_low, grad_key_low, grad_values_low], axis=1)
    all_grad_heads = lax.all_gather(grad_heads_all, "ep", axis=0, tiled=True)

    token_blocks, first_small = input_grad(
        grad_query_low,
        grad_key_low,
        grad_values_low,
        query_weight,
        key_matrix,
        value_matrix,
        own_columns(inputs),
        jnp.broadcast_to(first_scale[None, :], (8, ROWS)),
        vectors,
        grad_att_blocks,
    )
    grad_tokens = joined(token_blocks).astype(F32)
    grad_qkv_weight = contract_rows(all_normed, all_grad_heads)
    width = heads_local * HEAD_SIZE
    own_router = contract_rows(turn, small[:16])
    pieces = jnp.concatenate([own_router, small[16:18], first_small[:1]], axis=0)
    lines = jnp.concatenate(
        [
            pieces.reshape(-1),
            jnp.sum(grad_heads_all.astype(F32), axis=0),
            grad_sinks,
            jnp.sum(turn * jnp.sum(grad_logits, axis=1)[:, None], axis=0),
        ]
    )
    lines = lax.psum(lines, "ep")
    count = 19 * SHARE
    across = lax.all_gather(lines[:count].reshape(19, SHARE), "tp", axis=1, tiled=True)[:, :D]
    heads_sum = lines[count : count + width + 2 * HEAD_SIZE]
    rest = lines[count + width + 2 * HEAD_SIZE :]
    return (
        layer_output,
        grad_tokens,
        across[18],
        grad_qkv_weight[:, :width],
        grad_qkv_weight[:, width : width + HEAD_SIZE],
        grad_qkv_weight[:, width + HEAD_SIZE :],
        heads_sum[:width],
        heads_sum[width : width + HEAD_SIZE],
        heads_sum[width + HEAD_SIZE :],
        rest[:heads_local],
        grad_output_weight,
        across[17],
        across[16],
        across[:16].T,
        rest[heads_local:],
        grad_gateup[None],
        grad_gateup_bias,
        grad_down[None],
        grad_down_bias,
    )


def solution(mesh):
    in_specs = (
        P("ep", None),
        P(),
        P("ep", None),
        P(),
        P(None, "tp"),
        P(None, "tp"),
        P(None, "tp"),
        P("tp"),
        P("tp"),
        P("tp"),
        P("tp"),
        P("tp", None),
        P(),
        P(),
        P(),
        P(),
        P("ep", None, None, "tp"),
        P("ep", None, "tp"),
        P("ep", "tp", None),
        P("ep", None),
        P("ep", None),
    )
    out_specs = (
        P("ep", None),
        P("ep", None),
        P(),
        P(None, "tp"),
        P(None, "tp"),
        P(None, "tp"),
        P("tp"),
        P("tp"),
        P("tp"),
        P("tp"),
        P("tp", None),
        P(),
        P(),
        P(),
        P(),
        P("ep", None, None, "tp"),
        P("ep", None, "tp"),
        P("ep", "tp", None),
        P("ep", None),
    )
    return jax.shard_map(shards, mesh=mesh, in_specs=in_specs, out_specs=out_specs, check_vma=False)
```

time: 630 us -> 529 us (0.84)
  Pallas kernels: 0 us -> 181 us
  waiting for transfers between devices: 213 us -> 93.8 us
  blocking collectives: 148 us -> 85.1 us
  matrix products: 87.6 us -> 38.7 us
  other arithmetic: 45.5 us -> 14 us
  local copies, waits for them, and re-layouts: 108 us -> 89.2 us
    pallas_call x0 -> x4, Pallas kernels: none -> 181 us  [the longest x1 132 us: experts(): pl.pallas_call(expert_kernel, out_shape=(shape((8, SLOTS, SHARE), BF16),...]
    reduce_scatter x4 -> x0, waiting for transfers between devices: 91.6 us -> none  [the longest x2 58.6 us: send_home(): lax.psum_scatter(blocks, 'tp', scatter_dimension=1, tiled=True)]
    all_to_all x4 -> x0, blocking collectives: 73.1 us -> none  [the longest x2 37.5 us: send_home(): lax.all_to_all(shares, 'ep', split_axis=0, concat_axis=0, tiled=True)]
    dot_general x20 -> x11, matrix products: 48.4 us -> 6.11 us  [the longest x5 4.65 us: product(): return jnp.dot(left, right, preferred_element_type=F32)]
    psum x1 -> x0, waiting for transfers between devices: 40.5 us -> none  [shards(): lax.psum(grad_query_weight.astype(jnp.bfloat16), 'ep').astype(jnp.float32)]
    unnamed x209 -> x164, local copies, waits for them, and re-layouts: 22.7 us -> 59.7 us
    reshape x4, local copies, waits for them, and re-layouts: 21.6 us -> 1.58 us  [the longest x1 0.97 us: shards(): jnp.pad(cotangent, ((0, 0), (0, WIDE - D))).reshape(ROWS, BLOCKS, SHARE)]
    add x2 -> x0, local copies, waits for them, and re-layouts: 19.2 us -> none  [the longest x1 9.71 us: shards(): against_rows(grad_gate_low, expert_gateup[0, 0])]
  transfers between devices with their start and end apart: 10 -> 4, of which waited for: 8 -> 2; matrix products, arithmetic and copies ran while one was open for 21% -> 11% of each run, Pallas kernels for 0% -> 6%
where the time goes in v1:
time: 529 us; the launch traced here: 519 us
  Pallas kernels  181 us (34%)
  waiting for transfers between devices  93.8 us (18%)
  local copies, waits for them, and re-layouts  89.2 us (17%)
  blocking collectives  85.1 us (16%)
  matrix products  38.7 us (7%)
  between operations  16.5 us (3%)
  other arithmetic  14 us (3%)
    pallas_call x1, Pallas kernels, experts(): pl.pallas_call(expert_kernel, out_shape=(shape((8, SLOTS, SHARE), BF16),...  132 us
    all_gather x1, waiting for transfers between devices, shards(): all_grad_attended = lax.all_gather(grad_attended, 'ep', axis=0, tiled=True)  90.5 us
    unnamed x164, local copies, waits for them, and re-layouts  59.7 us
    psum x1, blocking collectives, shards(): lines = lax.psum(lines, 'ep')  58 us
    dot_general x3, matrix products, contract_rows(): lax.dot_general(left, right, (((0,), (0,)), ((), ())), preferred_element_...  30.1 us
    all_gather x1, blocking collectives, shards(): lax.all_gather(lines[:count].reshape(19, SHARE), 'tp', axis=1, tiled=True)  27.1 us
    pallas_call x1, Pallas kernels, input_grad(): pl.pallas_call(input_kernel, out_shape=(jax.ShapeDtypeStruct((8, ROWS, SH...  22 us
    pallas_call x1, Pallas kernels, attend_end(): pl.pallas_call(attend_kernel, out_shape=(jax.ShapeDtypeStruct((ROWS, SHAR...  16.8 us
  transfers between devices with their start and end apart: 4, of which 2 were waited for; matrix products, arithmetic and copies ran while one was open for 11% of the time, Pallas kernels for 6%

profile of v1, /device:TPU:1, one launch (start us, length us, event | category | flops | bytes accessed | tf_op | source)
XLA Modules:
  0.0 518.7 jit_solution(7025879638438675439)
XLA Ops:
  7.3 2.4 copy.130
  11.1 2.3 convert_element_type.129
  14.9 2.2 multiply_convert_fusion
  25.5 3.4 copy.137.weight
  39.1 2.3 copy.140
  45.1 6.3 %copy.142 = bf16[1,2,2880,360]{3,2,1,0:T(8,128)(2,1)} copy(bf16[1,2,2880,360]{2,3,1,0:T(8,128)(2,1)} %param.37) | data formatting | bytes 8294400 | tf_op args[16]
  51.4 3.3 pad.46.down
  56.0 16.8 %attend_end.1 = (bf16[128,384]{1,0:T(8,128)(2,1)S(1)}, f32[128,384]{1,0:T(8,128)S(1)}, f32[40,128]{1,0:T(8,128)S(1)}) custom-call(bf16[128,512]{1,0:T(8,128)(2,1)S(1)} %copy.136.heads, bf16[512,2880]{1,0:T(8,128)(2,1)S(1)} %copy.137.weight, f32[128,384]{1,0:T(8,128)S(1)} %pad_dynamic-slice_fusion.inputs, f32[8,384]{1,0:T(8,128)S(1)} %pad_dynamic-slice_fusion.2.vectors, ...), custom_call_target="tpu_custom_call" | custom-call | tf_op jit(solution)/shard_map/attend_end/pallas_call | solution.py:279
  74.7 131.6 %experts.1 = (bf16[8,768,384]{2,1,0:T(8,128)(2,1)}, bf16[8,768,384]{2,1,0:T(8,128)(2,1)}, bf16[768,360]{1,0:T(8,128)(2,1)}, bf16[768,360]{1,0:T(8,128)(2,1)}, bf...) custom-call(bf16[128,384]{1,0:T(8,128)(2,1)} %copy-done.15, ...), custom_call_target="tpu_custom_call" | custom-call | tf_op jit(solution)/shard_map/experts/pallas_call | solution.py:646
  214.6 2.5 convolution_convert_fusion.2
  223.9 2.1 copy.152.key_weight
  226.0 2.1 copy.153.value_weight
  231.5 22.0 %input_grad.1 = (bf16[8,128,384]{2,1,0:T(8,128)(2,1)S(1)}, f32[8,384]{1,0:T(8,128)S(1)}) custom-call(bf16[128,512]{1,0:T(8,128)(2,1)S(1)} %copy.150.grad_query, bf16[128,64]{1,0:T(8,128)(2,1)S(1)} %fusion.27.grad_key, bf16[128,64]{1,0:T(8,128)(2,1)S(1)} %copy.151.grad_value, bf16[2880,512]{1,0:T(8,128)(2,1)S(1)} %copy-done.3, ...), custom_call_target="tpu_custom_call" | custom-call | tf_op jit(solution)/shard_map/input_grad/pallas_call | solution.py:770
  255.3 58.0 %psum.7 = f32[7960]{0:T(1024)S(1)} all-reduce(f32[7960]{0:T(1024)S(1)} %concatenate.46), channel_id=1, replica_groups=mesh['ep'=16,'tp'=8] {'ep'}, use_global_device_ids=true, to_apply=%region_10.11 | all-reduce | flops 7960 | bytes 63680 | tf_op jit(solution)/shard_map/psum | solution.py:979
  324.9 3.0 copy.156
  328.0 2.4 copy-done.17
  330.4 2.4 copy-done.18
  332.8 10.7 %expert_grads.1 = (f32[2,2880,360]{2,1,0:T(8,128)}, f32[360,2880]{1,0:T(8,128)}, f32[8,8,384]{2,1,0:T(8,128)S(1)}) custom-call(bf16[8,768,384]{2,1,0:T(8,128)(2,1)S(1)} %copy-done.17, bf16[8,768,384]{2,1,0:T(8,128)(2,1)S(1)} %copy-done.18, bf16[768,360]{1,0:T(8,128)(2,1)S(1)} %copy-done.19, bf16[768,360]{1,0:T(8,128)(2,1)S(1)} %copy-done.9, ...), custom_call_target="tpu_custom_call" | custom-call | flops 4777574400 | bytes 22000000 | tf_op jit(solution)/shard_map/expert_grads/pallas_call | solution.py:707
  343.5 9.1 %copy.159 = f32[1,2,2880,360]{2,3,1,0:T(8,128)} copy(f32[1,2,2880,360]{3,2,1,0:T(8,128)} %bitcast.134) | data formatting | bytes 16588800
  353.6 27.1 %all_gather.15 = f32[19,3072]{1,0:T(8,128)S(1)} all-gather(f32[19,384]{1,0:T(8,128)S(1)} %reshape.449), channel_id=1, replica_groups=mesh['ep'=16,'tp'=8] {'tp'}, dimensions={1}, use_global_device_ids=true | all-gather | bytes 262656 | tf_op jit(solution)/shard_map/all_gather | solution.py:981
  383.2 14.0 %fusion.52 = f32[2880,640]{1,0:T(8,128)S(1)} fusion(bf16[2048,2880]{1,0:T(8,128)(2,1)} %all-gather.5.cloned.1.call-done, bf16[2048,640]{0,1:T(8,128)(2,1)} %all-gather.7.cloned.1.call-done), kind=kOutput, calls=%fused_computation.153 | convolution fusion | flops 7549747200 | bytes 21790720 | tf_op jit(solution)/shard_map/dot_general | solution.py:39
  397.2 3.4 slice.232
  405.6 90.5 %all-gather.11.cloned.1.call-done = bf16[2048,2880]{1,0:T(8,128)(2,1)} async-done(((bf16[128,2880]{1,0:T(8,128)(2,1)}), bf16[2048,2880]{1,0:T(8,128)(2,1)}) %all-gather.11.cloned.1.call-update) | async-done | bytes 11796496 | tf_op jit(solution)/shard_map/all_gather | solution.py:928
  496.1 15.9 %fusion.53 = f32[512,2880]{0,1:T(8,128)} fusion(bf16[2048,512]{0,1:T(8,128)(2,1)} %all-gather.9.cloned.1.call-done, bf16[2048,2880]{1,0:T(8,128)(2,1)} %all-gather.11.cloned.1.call-done), kind=kOutput, calls=%fused_computation.154 | convolution fusion | flops 6039797760 | bytes 19791872 | tf_op jit(solution)/shard_map/dot_general | solution.py:39
  (262 shorter events, 66.4 us)
Async XLA Ops:
  7.2 22.9 %copy-start = (bf16[2880,16]{0,1:T(8,128)(2,1)S(1)}, bf16[2880,16]{0,1:T(8,128)(2,1)}, u32[]{:S(2)}) copy-start(bf16[2880,16]{0,1:T(8,128)(2,1)} %param.35) | copy-start | bytes 276484
  7.2 7.7 %copy-start.43 = (f32[2880]{0:T(1024)S(1)}, f32[2880]{0:T(1024)}, u32[]{:S(2)}) copy-start(f32[2880]{0:T(1024)} %param.24) | copy-start | bytes 34564
  7.2 376.0 %all-gather.7.cloned.1.call-start = ((), (), s32[]{:S(2)}) async-start(), calls=%async_computation.1 | async-start | bytes 2785280 | tf_op jit(solution)/shard_map/all_gather | solution.py:952
  7.3 16.1 %copy-start.50 = (f32[32]{0:T(128)}, f32[32]{0:T(128)S(1)}, u32[]{:S(2)}) copy-start(f32[32]{0:T(128)S(1)} %negate_power_fusion) | copy-start | bytes 388
  7.3 9.9 %copy-start.2 = (bf16[2880,512]{1,0:T(8,128)(2,1)S(1)}, bf16[2880,512]{1,0:T(8,128)(2,1)}, u32[]{:S(2)}) copy-start(bf16[2880,512]{1,0:T(8,128)(2,1)} %query_weight.1) | copy-start | bytes 8847364
  7.3 9.9 %copy-start.55 = (f32[512]{0:T(512)S(1)}, f32[512]{0:T(512)}, u32[]{:S(2)}) copy-start(f32[512]{0:T(512)} %param.28) | copy-start | bytes 6148
  13.5 16.9 %copy-start.58 = (s32[16]{0:T(128)}, s32[16]{0:T(128)S(1)}, u32[]{:S(2)}) copy-start(s32[16]{0:T(128)S(1)} %fusion.36) | copy-start | bytes 196
  30.1 25.9 %copy-start.12 = (f32[8,384]{1,0:T(8,128)}, f32[8,384]{1,0:T(8,128)S(1)}, u32[]{:S(2)}) copy-start(f32[8,384]{1,0:T(8,128)S(1)} %pad_dynamic-slice_fusion.2.vectors) | copy-start | bytes 36868
  30.4 25.7 %copy-start.14 = (bf16[16,384]{1,0:T(8,128)(2,1)}, bf16[16,384]{1,0:T(8,128)(2,1)S(1)}, u32[]{:S(2)}) copy-start(bf16[16,384]{1,0:T(8,128)(2,1)S(1)} %pad_dynamic-slice_fusion.1.router) | copy-start | bytes 36868
  206.3 11.0 %copy-start.23 = (f32[8,128,128]{1,2,0:T(8,128)S(1)}, f32[8,128,128]{1,2,0:T(8,128)}, u32[]{:S(2)}) copy-start(f32[8,128,128]{1,2,0:T(8,128)} %copy-done.22) | copy-start | bytes 1572868
  206.4 11.0 %copy-start.28 = (f32[8,128]{1,0:T(8,128)S(1)}, f32[8,128]{1,0:T(8,128)}, u32[]{:S(2)}) copy-start(f32[8,128]{1,0:T(8,128)} %copy-done.27) | copy-start | bytes 12292
  206.4 11.0 %copy-start.30 = (bf16[128,64,1]{0,1,2:T(8,128)(2,1)S(1)}, bf16[128,64,1]{0,1,2:T(8,128)(2,1)}, u32[]{:S(2)}) copy-start(bf16[128,64,1]{0,1,2:T(8,128)(2,1)} %copy-done.29) | copy-start | bytes 49156
  219.8 8.3 %copy-start.57 = (f32[128]{0:T(128)S(1)}, f32[128]{0:T(128)}, u32[]{:S(2)}) copy-start(f32[128]{0:T(128)} %copy-done.56) | copy-start | bytes 1540
  219.8 8.3 %copy-start.3 = (bf16[2880,512]{1,0:T(8,128)(2,1)S(1)}, bf16[2880,512]{1,0:T(8,128)(2,1)}, u32[]{:S(2)}) copy-start(bf16[2880,512]{1,0:T(8,128)(2,1)} %query_weight.1) | copy-start | bytes 8847364
  219.8 8.3 %copy-start.13 = (f32[8,384]{1,0:T(8,128)S(1)}, f32[8,384]{1,0:T(8,128)}, u32[]{:S(2)}) copy-start(f32[8,384]{1,0:T(8,128)} %copy-done.12) | copy-start | bytes 36868
  219.8 163.3 %all-gather.5.cloned.1.call-start = ((), (), s32[]{:S(2)}) async-start(), calls=%async_computation | async-start | bytes 12812288 | tf_op jit(solution)/shard_map/all_gather | solution.py:875
  220.6 185.0 %all-gather.9.cloned.1.call-start = ((), (), s32[]{:S(2)}) async-start(), calls=%async_computation.2 | async-start | bytes 2228224 | tf_op jit(solution)/shard_map/all_gather | solution.py:901
  221.3 274.8 %all-gather.11.cloned.1.call-start = ((), (), s32[]{:S(2)}) async-start(), calls=%async_computation.3 | async-start | bytes 12812288 | tf_op jit(solution)/shard_map/all_gather | solution.py:928
  228.1 26.3 %copy-start.59 = (s32[16]{0:T(128)S(1)}, s32[16]{0:T(128)}, u32[]{:S(2)}) copy-start(s32[16]{0:T(128)} %copy-done.58) | copy-start | bytes 196
  228.1 26.6 %copy-start.53 = (f32[8]{0:T(128)S(1)}, f32[8]{0:T(128)}, u32[]{:S(2)}) copy-start(f32[8]{0:T(128)} %param.31) | copy-start | bytes 100
  231.5 22.9 %copy-start.64 = (f32[24,384]{1,0:T(8,128)S(1)}, f32[24,384]{1,0:T(8,128)}, u32[]{:S(2)}) copy-start(f32[24,384]{1,0:T(8,128)} %get-tuple-element.43) | copy-start | bytes 110596
  231.5 23.4 %copy-start.49 = (f32[16,128]{1,0:T(8,128)S(1)}, f32[16,128]{1,0:T(8,128)}, u32[]{:S(2)}) copy-start(f32[16,128]{1,0:T(8,128)} %get-tuple-element.45) | copy-start | bytes 24580
  254.5 69.0 %copy-start.8 = (bf16[8,128,384]{2,1,0:T(8,128)(2,1)S(1)}, bf16[8,128,384]{2,1,0:T(8,128)(2,1)}, u32[]{:S(2)}) copy-start(bf16[8,128,384]{2,1,0:T(8,128)(2,1)} %copy-done.7) | copy-start | bytes 2359300
  496.1 15.9 %copy-start.1 = (bf16[2880,16]{0,1:T(8,128)(2,1)S(1)}, bf16[2880,16]{0,1:T(8,128)(2,1)}, u32[]{:S(2)}) copy-start(bf16[2880,16]{0,1:T(8,128)(2,1)} %param.35) | copy-start | bytes 276484
  (46 other events, 142.7 us)
Sparse Core Ops, SparseCore 0:
  220.0 46.3 all-gather.6
  269.1 88.0 all-gather.4
  359.3 46.2 all-gather.8
  408.2 87.8 all-gather.10
